TPU v7x, 32 devices: a whole 2x2x4 slice. The times are simulated.
32 devices in a mesh: ctx: 16 (over z, y, core), wt: 2 (over x).
Axes of the slice: x: 2, y: 2, z: 4, core: 2. Of those that a mesh axis runs over, the one named last changes fastest.
Arguments:
- inputs: bfloat16 [6144, 1472], P('ctx'), may hold values from -24 to 24
- delete_mask: bfloat16 [6144], P('ctx'), may hold values from -4 to 0
- lengths: int32 [6], replicated, may hold values from 1024 to 1024, as said below
- dealing: int32 [6144], replicated, may hold values from 0 to 6143, as said below
- w_query: bfloat16 [1472, 384], P(None, 'wt'), may hold values from -0.0390625 to 0.0390625
- w_key: bfloat16 [1472, 384], P(None, 'wt'), may hold values from -0.15625 to 0.15625
- w_value: bfloat16 [1472, 384], P(None, 'wt'), may hold values from -0.15625 to 0.15625
- w_output: bfloat16 [384, 1472], P('wt'), may hold values from -0.875 to 0.875
- bias_table: float32 [32, 6], P(None, 'wt'), may hold values from -4 to 4
- norm_attn: float32 [1472], replicated, may hold values from 0.5 to 1.5
- w_gate: bfloat16 [1472, 3584], P(None, 'wt'), may hold values from -0.15625 to 0.15625
- w_up: bfloat16 [1472, 3584], P(None, 'wt'), may hold values from -0.15625 to 0.15625
- w_down: bfloat16 [3584, 1472], P('wt'), may hold values from -0.09375 to 0.09375
- norm_ffn: float32 [1472], replicated, may hold values from 0.5 to 1.5
- out_grad: bfloat16 [6144, 1472], P('ctx'), may hold values from -6 to 6
Outputs:
- output: bfloat16 [6144, 1472], P('ctx')
- input_grad: bfloat16 [6144, 1472], P('ctx')
- mask_grad: bfloat16 [6144], P('ctx')
- grad_query: float32 [1472, 384], P('ctx', 'wt')
- grad_key: float32 [1472, 384], P('ctx', 'wt')
- grad_value: float32 [1472, 384], P('ctx', 'wt')
- grad_output: float32 [384, 1472], P('wt', 'ctx')
- grad_table: float32 [32, 6], P(None, 'wt')
- grad_norm_attn: float32 [1472], P('ctx')
- grad_gate: float32 [1472, 3584], P('ctx', 'wt')
- grad_up: float32 [1472, 3584], P('ctx', 'wt')
- grad_down: float32 [3584, 1472], P('wt', 'ctx')
- grad_norm_ffn: float32 [1472], P('ctx')
- root_means: float32 [3], replicated
Inputs may be any that keep to these rules, and one draw needn't show every extreme that they name: Sequence s takes the tokens from the sum of the earlier lengths on; the lengths sum to 6144; in every draw one sequence has exactly 1024 tokens and one exactly 1024. `dealing`: A permutation of the tokens. The 384 dealt slots of each index of ctx take exactly 24 tokens from each block of 384 consecutive tokens, the blocks in order, so slot c * 384 + b * 24 + m holds a token of block b.
All inputs are finite; a program needn't handle non-finite values.
Results may differ from a plain program's by a relative error of at most 0.018.
Values may be sent and summed in bfloat16 or wider, within the bound.
A program may use at most 256 MiB of HBM per device.

v0:
```python
from functools import partial

import jax
import jax.numpy as jnp
from jax import lax
from jax.sharding import PartitionSpec as P

HD = 64


THRESHOLDS = (1, 2, 3, 4, 5, 6, 7, 8, 12, 16, 23, 32, 46, 64, 91)
MASKED = -1e30
EPSILON = 1e-06


def bucket_of(offset):
    distance = jnp.abs(offset)
    bucket_sum = (offset > 0).astype(jnp.int32) * 16
    for threshold in THRESHOLDS:
        bucket_sum = bucket_sum + (distance >= threshold).astype(jnp.int32)
    return bucket_sum


def places(initial, lengths):
    starts = jnp.cumsum(lengths) - lengths
    inside = initial[:, None] >= starts[None, :]
    sequence = jnp.sum(inside.astype(jnp.int32), axis=1) - 1
    opening = jnp.max(jnp.where(inside, starts[None, :], 0), axis=1)
    return (sequence, initial - opening)


def mat_t(left_side, right_side):
    return lax.dot_general(
        left_side, right_side, (((1,), (1,)), ((), ())), preferred_element_type=jnp.float32
    )


def t_mat(left_side, right_side):
    return lax.dot_general(
        left_side, right_side, (((0,), (0,)), ((), ())), preferred_element_type=jnp.float32
    )


def norm_back(grad_in, normed, inverse, gain_in):
    scaled = grad_in * gain_in
    return inverse * (scaled - normed * jnp.mean(scaled * normed, axis=-1, keepdims=True))


def pair_terms(table_here, query_seq, query_pos, key_seq, key_pos, key_mask):
    bucket = bucket_of(key_pos[None, :] - query_pos[:, None])
    bucket_ids = jnp.arange(table_here.shape[0], dtype=jnp.int32)
    chosen = bucket[None, :, :, None] == bucket_ids[None, None, None, :]
    table_heads = jnp.transpose(table_here)[:, None, None, :]
    added_terms = jnp.sum(jnp.where(chosen, table_heads, 0.0), axis=-1)
    added_terms = added_terms + key_mask.astype(jnp.float32)[None, None, :]
    same_seq = key_seq[None, :] == query_seq[:, None]
    return (added_terms, same_seq, chosen)


def score_block(query_heads, key_heads, added_terms, same_seq):
    raw_score = jnp.einsum(
        "qhd,khd->hqk", query_heads, key_heads, preferred_element_type=jnp.float32
    )
    return jnp.where(same_seq[None], raw_score + added_terms, MASKED)


def table_sums(score_grad, chosen):
    summed = jnp.sum(jnp.where(chosen, score_grad[..., None], 0.0), axis=(1, 2))
    return jnp.transpose(summed)


def grad_block(
    table_here,
    query_part,
    grad_part,
    top_part,
    delta_part,
    query_seq,
    query_pos,
    key_heads,
    value_heads,
    key_seq,
    key_pos,
    key_mask,
):
    added_terms, same_seq, chosen = pair_terms(
        table_here, query_seq, query_pos, key_seq, key_pos, key_mask
    )
    probs_here = jnp.exp(
        score_block(query_part, key_heads, added_terms, same_seq) - top_part[..., None]
    )
    prob_grad = jnp.einsum(
        "qhd,khd->hqk", grad_part, value_heads, preferred_element_type=jnp.float32
    )
    score_grad = probs_here * (prob_grad - delta_part[..., None])
    return (probs_here, score_grad, chosen)


def local(
    inputs,
    delete_mask,
    lengths,
    dealing,
    w_query,
    w_key,
    w_value,
    w_output,
    bias_table,
    norm_attn,
    w_gate,
    w_up,
    w_down,
    norm_ffn,
    out_grad,
):
    tok_here = inputs.shape[0]
    model_width = inputs.shape[1]
    ctx_count = lax.axis_size("ctx")
    ctx_rank = lax.axis_index("ctx")
    quota_each = tok_here // ctx_count
    tokens_all = tok_here * ctx_count
    heads_here = w_query.shape[1] // HD
    head_cols = heads_here * HD
    grouped = dealing.reshape(ctx_count, ctx_count, quota_each)
    sent_rows = (
        lax.dynamic_index_in_dim(grouped, ctx_rank, 1, keepdims=False).reshape(tok_here)
        - ctx_rank * tok_here
    )
    outgoing = (
        jnp.take(inputs, sent_rows, axis=0),
        jnp.take(out_grad, sent_rows, axis=0),
        jnp.take(delete_mask, sent_rows, axis=0),
    )
    dealt_x, dealt_grad, dealt_mask = (
        lax.all_to_all(outgoing[0], "ctx", split_axis=0, concat_axis=0, tiled=True),
        lax.all_to_all(outgoing[1], "ctx", split_axis=0, concat_axis=0, tiled=True),
        lax.all_to_all(outgoing[2], "ctx", split_axis=0, concat_axis=0, tiled=True),
    )
    seq_all, pos_all = places(dealing, lengths)
    query_seq = lax.dynamic_slice_in_dim(seq_all, ctx_rank * tok_here, tok_here)
    query_pos = lax.dynamic_slice_in_dim(pos_all, ctx_rank * tok_here, tok_here)
    stream_in = dealt_x.astype(jnp.float32)
    inverse_one = lax.rsqrt(jnp.mean(stream_in * stream_in, axis=-1, keepdims=True) + EPSILON)
    normed_one = stream_in * inverse_one
    hidden_one = (normed_one * norm_attn).astype(jnp.bfloat16)
    queries = jnp.dot(hidden_one, w_query, preferred_element_type=jnp.float32).astype(jnp.bfloat16)
    keys_here = jnp.dot(hidden_one, w_key, preferred_element_type=jnp.float32).astype(jnp.bfloat16)
    values_here = jnp.dot(hidden_one, w_value, preferred_element_type=jnp.float32).astype(
        jnp.bfloat16
    )
    keys_all, values_all, mask_all = (
        lax.all_gather(keys_here, "ctx", axis=0, tiled=True),
        lax.all_gather(values_here, "ctx", axis=0, tiled=True),
        lax.all_gather(dealt_mask, "ctx", axis=0, tiled=True),
    )
    block_rows = 2 * tok_here
    block_count = tokens_all // block_rows
    key_blocks = keys_all.reshape(block_count, block_rows, heads_here, HD)
    value_blocks = values_all.reshape(block_count, block_rows, heads_here, HD)
    seq_blocks = seq_all.reshape(block_count, block_rows)
    pos_blocks = pos_all.reshape(block_count, block_rows)
    mask_blocks = mask_all.reshape(block_count, block_rows)
    query_heads = queries.reshape(tok_here, heads_here, HD)

    def top_step(state_in, block_in):
        running_top, running_sum = state_in
        key_heads, key_seq, key_pos, key_mask = block_in
        added_terms, same_seq, chosen = pair_terms(
            bias_table, query_seq, query_pos, key_seq, key_pos, key_mask
        )
        scores = score_block(query_heads, key_heads, added_terms, same_seq)
        new_top = jnp.maximum(running_top, jnp.max(scores, axis=-1))
        running_sum = running_sum * jnp.exp(running_top - new_top) + jnp.sum(
            jnp.exp(scores - new_top[..., None]), axis=-1
        )
        return ((new_top, running_sum), None)

    start_top = jnp.full((heads_here, tok_here), MASKED, jnp.float32)
    start_sum = jnp.zeros((heads_here, tok_here), jnp.float32)
    (final_top, final_sum), unused = lax.scan(
        top_step, (start_top, start_sum), (key_blocks, seq_blocks, pos_blocks, mask_blocks)
    )
    log_total = final_top + jnp.log(final_sum)

    def value_step(state_in, block_in):
        high_sum, low_sum = state_in
        key_heads, value_heads, key_seq, key_pos, key_mask = block_in
        added_terms, same_seq, chosen = pair_terms(
            bias_table, query_seq, query_pos, key_seq, key_pos, key_mask
        )
        probs_here = jnp.exp(
            score_block(query_heads, key_heads, added_terms, same_seq) - log_total[..., None]
        )
        probs_high = probs_here.astype(jnp.bfloat16)
        probs_rest = (probs_here - probs_high.astype(jnp.float32)).astype(jnp.bfloat16)
        high_sum = high_sum + jnp.einsum(
            "hqk,khd->qhd", probs_high, value_heads, preferred_element_type=jnp.float32
        )
        low_sum = low_sum + jnp.einsum(
            "hqk,khd->qhd", probs_rest, value_heads, preferred_element_type=jnp.float32
        )
        return ((high_sum, low_sum), None)

    zero_heads = jnp.zeros((tok_here, heads_here, HD), jnp.float32)
    all_blocks = (key_blocks, value_blocks, seq_blocks, pos_blocks, mask_blocks)
    (high_total, low_total), unused = lax.scan(value_step, (zero_heads, zero_heads), all_blocks)
    attended = high_total.reshape(tok_here, head_cols).astype(jnp.bfloat16)
    exact_out = high_total + low_total
    branch_attn = lax.psum(
        jnp.dot(attended, w_output, preferred_element_type=jnp.float32).astype(jnp.bfloat16), "wt"
    ).astype(jnp.float32)
    stream_mid = stream_in + branch_attn
    inverse_two = lax.rsqrt(jnp.mean(stream_mid * stream_mid, axis=-1, keepdims=True) + EPSILON)
    normed_two = stream_mid * inverse_two
    hidden_two = (normed_two * norm_ffn).astype(jnp.bfloat16)
    gate_value = jnp.dot(hidden_two, w_gate, preferred_element_type=jnp.float32)
    up_value = jnp.dot(hidden_two, w_up, preferred_element_type=jnp.float32)

    def gated_unit(gate_in, up_in):
        return jax.nn.gelu(gate_in, approximate=True) * up_in

    activated, gated_pull = jax.vjp(gated_unit, gate_value, up_value)
    inner_low = activated.astype(jnp.bfloat16)
    branch_ffn = lax.psum(
        jnp.dot(inner_low, w_down, preferred_element_type=jnp.float32).astype(jnp.bfloat16), "wt"
    ).astype(jnp.float32)
    stream_out = stream_mid + branch_ffn
    squares = jnp.stack(
        [
            jnp.sum(stream_out * stream_out),
            jnp.sum(branch_attn * branch_attn),
            jnp.sum(branch_ffn * branch_ffn),
        ]
    )
    inner_grad = mat_t(dealt_grad, w_down)
    gate_grad, up_grad = gated_pull(inner_grad)
    gate_low = gate_grad.astype(jnp.bfloat16)
    up_low = up_grad.astype(jnp.bfloat16)
    hidden_two_grad = lax.psum(
        (mat_t(gate_low, w_gate) + mat_t(up_low, w_up)).astype(jnp.bfloat16), "wt"
    ).astype(jnp.float32)
    gain_two_grad = jnp.sum(hidden_two_grad * normed_two, axis=0)
    stream_mid_grad = dealt_grad.astype(jnp.float32) + norm_back(
        hidden_two_grad, normed_two, inverse_two, norm_ffn
    )
    attn_grad_low = stream_mid_grad.astype(jnp.bfloat16)
    attended_grad = mat_t(attn_grad_low, w_output).astype(jnp.bfloat16)
    grad_heads = attended_grad.reshape(tok_here, heads_here, HD)
    row_delta = jnp.transpose(jnp.sum(grad_heads.astype(jnp.float32) * exact_out, axis=-1))

    def backward_step(with_keys, state_in, block_in):
        query_acc, table_acc = state_in
        key_heads, value_heads, key_seq, key_pos, key_mask = block_in
        probs_here, score_grad, chosen = grad_block(
            bias_table,
            query_heads,
            grad_heads,
            log_total,
            row_delta,
            query_seq,
            query_pos,
            key_heads,
            value_heads,
            key_seq,
            key_pos,
            key_mask,
        )
        score_low = score_grad.astype(jnp.bfloat16)
        query_acc = query_acc + jnp.einsum(
            "hqk,khd->qhd", score_low, key_heads, preferred_element_type=jnp.float32
        )
        table_acc = table_acc + table_sums(score_grad, chosen)
        emitted = None
        emitted = (
            jnp.einsum("hqk,qhd->khd", score_low, query_heads, preferred_element_type=jnp.float32),
            jnp.einsum(
                "hqk,qhd->khd",
                probs_here.astype(jnp.bfloat16),
                grad_heads,
                preferred_element_type=jnp.float32,
            ),
            jnp.sum(score_grad, axis=(0, 1)),
        )
        return ((query_acc, table_acc), emitted)

    start_state = (zero_heads, jnp.zeros((bias_table.shape[0], heads_here), jnp.float32))
    (query_acc, table_acc), emitted = lax.scan(
        partial(backward_step, True), start_state, all_blocks
    )
    key_parts, value_parts, mask_parts = emitted
    key_grad, value_grad, mask_part = (
        lax.psum_scatter(
            key_parts.reshape(tokens_all, head_cols), "ctx", scatter_dimension=0, tiled=True
        ),
        lax.psum_scatter(
            value_parts.reshape(tokens_all, head_cols), "ctx", scatter_dimension=0, tiled=True
        ),
        lax.psum_scatter(mask_parts.reshape(tokens_all), "ctx", scatter_dimension=0, tiled=True),
    )
    query_low = query_acc.reshape(tok_here, head_cols).astype(jnp.bfloat16)
    key_low = key_grad.astype(jnp.bfloat16)
    value_low = value_grad.astype(jnp.bfloat16)
    hidden_one_part = mat_t(query_low, w_query) + mat_t(key_low, w_key) + mat_t(value_low, w_value)
    hidden_one_grad, mask_sum = (
        lax.psum(hidden_one_part.astype(jnp.bfloat16), "wt").astype(jnp.float32),
        lax.psum(mask_part.astype(jnp.bfloat16), "wt").astype(jnp.float32),
    )
    gain_one_grad = jnp.sum(hidden_one_grad * normed_one, axis=0)
    input_grad_here = stream_mid_grad + norm_back(
        hidden_one_grad, normed_one, inverse_one, norm_attn
    )
    weight_parts = (
        lax.psum_scatter(t_mat(hidden_one, query_low), "ctx", scatter_dimension=0, tiled=True),
        lax.psum_scatter(t_mat(hidden_one, key_low), "ctx", scatter_dimension=0, tiled=True),
        lax.psum_scatter(t_mat(hidden_one, value_low), "ctx", scatter_dimension=0, tiled=True),
        lax.psum_scatter(t_mat(attn_grad_low, attended), "ctx", scatter_dimension=0, tiled=True),
        lax.psum_scatter(t_mat(hidden_two, gate_low), "ctx", scatter_dimension=0, tiled=True),
        lax.psum_scatter(t_mat(hidden_two, up_low), "ctx", scatter_dimension=0, tiled=True),
        lax.psum_scatter(t_mat(dealt_grad, inner_low), "ctx", scatter_dimension=0, tiled=True),
        lax.psum_scatter(gain_one_grad, "ctx", scatter_dimension=0, tiled=True),
        lax.psum_scatter(gain_two_grad, "ctx", scatter_dimension=0, tiled=True),
    )
    table_grad, square_sum = lax.psum((table_acc, squares), "ctx")
    root_means = jnp.sqrt(square_sum / (tokens_all * model_width))
    back_out, back_grad = (
        lax.all_to_all(
            stream_out.astype(jnp.bfloat16), "ctx", split_axis=0, concat_axis=0, tiled=True
        ),
        lax.all_to_all(
            input_grad_here.astype(jnp.bfloat16), "ctx", split_axis=0, concat_axis=0, tiled=True
        ),
    )
    output_rows = jnp.zeros((tok_here, model_width), jnp.bfloat16).at[sent_rows].set(back_out)
    grad_rows = jnp.zeros((tok_here, model_width), jnp.bfloat16).at[sent_rows].set(back_grad)
    return (
        output_rows,
        grad_rows,
        mask_sum.astype(jnp.bfloat16),
        weight_parts[0],
        weight_parts[1],
        weight_parts[2],
        jnp.transpose(weight_parts[3]),
        table_grad,
        weight_parts[7],
        weight_parts[4],
        weight_parts[5],
        jnp.transpose(weight_parts[6]),
        weight_parts[8],
        root_means,
    )


def solution(mesh):
    return jax.shard_map(
        local,
        mesh=mesh,
        in_specs=(
            P("ctx", None),
            P("ctx"),
            P(),
            P(),
            P(None, "wt"),
            P(None, "wt"),
            P(None, "wt"),
            P("wt", None),
            P(None, "wt"),
            P(),
            P(None, "wt"),
            P(None, "wt"),
            P("wt", None),
            P(),
            P("ctx", None),
        ),
        out_specs=(
            P("ctx", None),
            P("ctx", None),
            P("ctx"),
            P("ctx", "wt"),
            P("ctx", "wt"),
            P("ctx", "wt"),
            P("wt", "ctx"),
            P(None, "wt"),
            P("ctx"),
            P("ctx", "wt"),
            P("ctx", "wt"),
            P("wt", "ctx"),
            P("ctx"),
            P(),
        ),
        check_vma=False,
    )
```

profile of v0, /device:TPU:0, one launch (start us, length us, event | category | flops | bytes accessed | tf_op | source)
XLA Modules:
  0.0 3060.0 jit_solution(6830339188608747822)
XLA Ops:
  20.9 36.7 %all_to_all.54 = bf16[16,24,1472]{2,1,0:T(8,128)(2,1)S(1)} all-to-all(bf16[16,24,1472]{2,1,0:T(8,128)(2,1)S(1)} %bitcast.238), channel_id=1, replica_groups=mesh['ctx'=16,'wt'=2] {'ctx'}, dimensions={0} | all-to-all | bytes 2260992 | tf_op jit(solution)/shard_map/all_to_all | solution.py:135
  79.1 18.1 all-gather
  109.6 39.1 %all-gather.6.cloned.1.call-done = bf16[6144,192]{0,1:T(8,128)(2,1)} async-done(((bf16[384,192]{0,1:T(8,128)(2,1)}), bf16[6144,192]{0,1:T(8,128)(2,1)}) %all-gather.6.cloned.1.call-update) | async-done | bytes 2359312 | tf_op jit(solution)/shard_map/all_gather | solution.py:152
  152.9 495.2 %while.45 = (s32[]{:T(128)}, f32[3,384]{1,0:T(4,128)S(1)}, f32[3,384]{1,0:T(4,128)S(1)}, s32[8,768]{1,0:T(8,128)S(1)}, s32[384]{0:T(512)S(1)}, /*index=5*/bf16[8...) while((s32[]{:T(128)}, f32[3,384]{1,0:T(4,128)S(1)}, ...), condition=%wide.region_8.10_spmd.clone, body=%wide.region_4.9_spmd.clone.sunk | while | flops 198482304 | bytes 43589144 | solution.py:180
  161.3 44.6 %select_reduce_fusion.8 = f32[3,384,768]{2,1,0:T(8,128)} fusion(f32[3,32]{1,0:T(4,128)S(1)} %bitcast.249, pred[384,768,32]{1,2,0:T(8,128)(4,1)} %iota_compare_fusion.6), kind=kLoop, calls=%fused_computation.5.clone.1 | loop fusion | flops 55738368 | bytes 12976512 | tf_op jit(solution)/shard_map/while/body/eval_jaxpr/reduce_sum | solution.py:54
  223.2 44.6 %select_reduce_fusion.8 = f32[3,384,768]{2,1,0:T(8,128)} fusion(f32[3,32]{1,0:T(4,128)S(1)} %bitcast.249, pred[384,768,32]{1,2,0:T(8,128)(4,1)} %iota_compare_fusion.6), kind=kLoop, calls=%fused_computation.5.clone.1 | loop fusion | flops 55738368 | bytes 12976512 | tf_op jit(solution)/shard_map/while/body/eval_jaxpr/reduce_sum | solution.py:54
  285.2 44.6 %select_reduce_fusion.8 = f32[3,384,768]{2,1,0:T(8,128)} fusion(f32[3,32]{1,0:T(4,128)S(1)} %bitcast.249, pred[384,768,32]{1,2,0:T(8,128)(4,1)} %iota_compare_fusion.6), kind=kLoop, calls=%fused_computation.5.clone.1 | loop fusion | flops 55738368 | bytes 12976512 | tf_op jit(solution)/shard_map/while/body/eval_jaxpr/reduce_sum | solution.py:54
  347.1 44.6 %select_reduce_fusion.8 = f32[3,384,768]{2,1,0:T(8,128)} fusion(f32[3,32]{1,0:T(4,128)S(1)} %bitcast.249, pred[384,768,32]{1,2,0:T(8,128)(4,1)} %iota_compare_fusion.6), kind=kLoop, calls=%fused_computation.5.clone.1 | loop fusion | flops 55738368 | bytes 12976512 | tf_op jit(solution)/shard_map/while/body/eval_jaxpr/reduce_sum | solution.py:54
  409.0 44.6 %select_reduce_fusion.8 = f32[3,384,768]{2,1,0:T(8,128)} fusion(f32[3,32]{1,0:T(4,128)S(1)} %bitcast.249, pred[384,768,32]{1,2,0:T(8,128)(4,1)} %iota_compare_fusion.6), kind=kLoop, calls=%fused_computation.5.clone.1 | loop fusion | flops 55738368 | bytes 12976512 | tf_op jit(solution)/shard_map/while/body/eval_jaxpr/reduce_sum | solution.py:54
  470.9 44.6 %select_reduce_fusion.8 = f32[3,384,768]{2,1,0:T(8,128)} fusion(f32[3,32]{1,0:T(4,128)S(1)} %bitcast.249, pred[384,768,32]{1,2,0:T(8,128)(4,1)} %iota_compare_fusion.6), kind=kLoop, calls=%fused_computation.5.clone.1 | loop fusion | flops 55738368 | bytes 12976512 | tf_op jit(solution)/shard_map/while/body/eval_jaxpr/reduce_sum | solution.py:54
  532.8 44.6 %select_reduce_fusion.8 = f32[3,384,768]{2,1,0:T(8,128)} fusion(f32[3,32]{1,0:T(4,128)S(1)} %bitcast.249, pred[384,768,32]{1,2,0:T(8,128)(4,1)} %iota_compare_fusion.6), kind=kLoop, calls=%fused_computation.5.clone.1 | loop fusion | flops 55738368 | bytes 12976512 | tf_op jit(solution)/shard_map/while/body/eval_jaxpr/reduce_sum | solution.py:54
  594.7 44.6 %select_reduce_fusion.8 = f32[3,384,768]{2,1,0:T(8,128)} fusion(f32[3,32]{1,0:T(4,128)S(1)} %bitcast.249, pred[384,768,32]{1,2,0:T(8,128)(4,1)} %iota_compare_fusion.6), kind=kLoop, calls=%fused_computation.5.clone.1 | loop fusion | flops 55738368 | bytes 12976512 | tf_op jit(solution)/shard_map/while/body/eval_jaxpr/reduce_sum | solution.py:54
  648.1 523.5 %while.46 = (s32[]{:T(128)}, f32[384,3,64]{0,2,1:T(8,128)}, f32[384,3,64]{0,2,1:T(8,128)}, bf16[8,768,3,64]{1,3,2,0:T(8,128)(2,1)}, s32[8,768]{1,0:T(8,128)S(1)}...) while((s32[]{:T(128)}, f32[384,3,64]{0,2,1:T(8,128)}, ...), condition=%wide.region_11.13_spmd.clone, body=%wide.region_9.12_spmd.clone.sunk | while | flops 427918080 | bytes 53560992 | solution.py:206
  656.8 44.6 %select_reduce_fusion.9 = f32[3,384,768]{2,1,0:T(8,128)} fusion(f32[3,32]{1,0:T(4,128)S(1)} %bitcast.250, pred[384,768,32]{1,2,0:T(8,128)(4,1)} %iota_compare_fusion.7), kind=kLoop, calls=%fused_computation.38.clone.1 | loop fusion | flops 55738368 | bytes 12976512 | tf_op jit(solution)/shard_map/while/body/eval_jaxpr/reduce_sum | solution.py:54
  722.2 44.6 %select_reduce_fusion.9 = f32[3,384,768]{2,1,0:T(8,128)} fusion(f32[3,32]{1,0:T(4,128)S(1)} %bitcast.250, pred[384,768,32]{1,2,0:T(8,128)(4,1)} %iota_compare_fusion.7), kind=kLoop, calls=%fused_computation.38.clone.1 | loop fusion | flops 55738368 | bytes 12976512 | tf_op jit(solution)/shard_map/while/body/eval_jaxpr/reduce_sum | solution.py:54
  787.7 44.6 %select_reduce_fusion.9 = f32[3,384,768]{2,1,0:T(8,128)} fusion(f32[3,32]{1,0:T(4,128)S(1)} %bitcast.250, pred[384,768,32]{1,2,0:T(8,128)(4,1)} %iota_compare_fusion.7), kind=kLoop, calls=%fused_computation.38.clone.1 | loop fusion | flops 55738368 | bytes 12976512 | tf_op jit(solution)/shard_map/while/body/eval_jaxpr/reduce_sum | solution.py:54
  853.1 44.6 %select_reduce_fusion.9 = f32[3,384,768]{2,1,0:T(8,128)} fusion(f32[3,32]{1,0:T(4,128)S(1)} %bitcast.250, pred[384,768,32]{1,2,0:T(8,128)(4,1)} %iota_compare_fusion.7), kind=kLoop, calls=%fused_computation.38.clone.1 | loop fusion | flops 55738368 | bytes 12976512 | tf_op jit(solution)/shard_map/while/body/eval_jaxpr/reduce_sum | solution.py:54
  918.5 44.6 %select_reduce_fusion.9 = f32[3,384,768]{2,1,0:T(8,128)} fusion(f32[3,32]{1,0:T(4,128)S(1)} %bitcast.250, pred[384,768,32]{1,2,0:T(8,128)(4,1)} %iota_compare_fusion.7), kind=kLoop, calls=%fused_computation.38.clone.1 | loop fusion | flops 55738368 | bytes 12976512 | tf_op jit(solution)/shard_map/while/body/eval_jaxpr/reduce_sum | solution.py:54
  983.9 44.6 %select_reduce_fusion.9 = f32[3,384,768]{2,1,0:T(8,128)} fusion(f32[3,32]{1,0:T(4,128)S(1)} %bitcast.250, pred[384,768,32]{1,2,0:T(8,128)(4,1)} %iota_compare_fusion.7), kind=kLoop, calls=%fused_computation.38.clone.1 | loop fusion | flops 55738368 | bytes 12976512 | tf_op jit(solution)/shard_map/while/body/eval_jaxpr/reduce_sum | solution.py:54
  1049.3 44.6 %select_reduce_fusion.9 = f32[3,384,768]{2,1,0:T(8,128)} fusion(f32[3,32]{1,0:T(4,128)S(1)} %bitcast.250, pred[384,768,32]{1,2,0:T(8,128)(4,1)} %iota_compare_fusion.7), kind=kLoop, calls=%fused_computation.38.clone.1 | loop fusion | flops 55738368 | bytes 12976512 | tf_op jit(solution)/shard_map/while/body/eval_jaxpr/reduce_sum | solution.py:54
  1114.7 44.6 %select_reduce_fusion.9 = f32[3,384,768]{2,1,0:T(8,128)} fusion(f32[3,32]{1,0:T(4,128)S(1)} %bitcast.250, pred[384,768,32]{1,2,0:T(8,128)(4,1)} %iota_compare_fusion.7), kind=kLoop, calls=%fused_computation.38.clone.1 | loop fusion | flops 55738368 | bytes 12976512 | tf_op jit(solution)/shard_map/while/body/eval_jaxpr/reduce_sum | solution.py:54
  1179.0 36.0 %all-reduce.24.cloned.1.call-done = bf16[384,1472]{0,1:T(8,128)(2,1)} async-done(((bf16[384,1472]{0,1:T(8,128)(2,1)}), bf16[384,1472]{0,1:T(8,128)(2,1)}) %all-reduce.24.cloned.1.call-update) | async-done | bytes 1130512 | tf_op jit(solution)/shard_map/psum | solution.py:209
  1229.9 8.4 multiply_convert_fusion
  1258.2 64.2 %all-reduce.28.cloned.1.call-done = (bf16[384,1472]{0,1:T(8,128)(2,1)}, bf16[384,1472]{0,1:T(8,128)(2,1)}) async-done(((bf16[384,1472]{0,1:T(8,128)(2,1)}, bf16[384,1472]{0,1:T(8,128)(2,1)}), (bf16[384,1472]{0,1:T(8,128)(2,1)}, bf16[384,1472]{0,1:T(8,128)(2,1)})) %all-reduce.28.cloned.1.call-update) | async-done | bytes 2261008 | tf_op jit(solution)/shard_map/psum | solution.py:224
  1331.1 947.3 %while.47 = (s32[]{:T(128)}, f32[384,3,64]{0,2,1:T(8,128)}, f32[32,3]{0,1:T(4,128)}, f32[8,768,3,64]{1,0,3,2:T(8,128)}, f32[8,768,3,64]{1,0,3,2:T(8,128)}, /*ind...) while((s32[]{:T(128)}, f32[384,3,64]{0,2,1:T(8,128)}, ...), condition=%wide.region_23.25_spmd.clone, body=%wide.region_19.24_spmd.clone.sunk | while | flops 711770240 | bytes 104671168 | solution.py:287
  1339.3 46.7 %select_reduce_fusion.10 = f32[3,384,768]{2,1,0:T(8,128)} fusion(f32[3,32]{1,0:T(4,128)S(1)} %bitcast.251, pred[384,768,32]{1,2,0:T(8,128)(4,1)S(1)} %iota_compare_fusion.8), kind=kLoop, calls=%fused_computation.84.clone.1 | loop fusion | flops 55738368 | bytes 12976512 | tf_op jit(solution)/shard_map/while/body/eval_jaxpr/reduce_sum | solution.py:54
  1393.8 23.7 select_reduce_fusion.11
  1423.9 12.5 dynamic_update_slice.17
  1436.5 12.5 dynamic_update_slice.18
  1457.1 46.7 %select_reduce_fusion.10 = f32[3,384,768]{2,1,0:T(8,128)} fusion(f32[3,32]{1,0:T(4,128)S(1)} %bitcast.251, pred[384,768,32]{1,2,0:T(8,128)(4,1)S(1)} %iota_compare_fusion.8), kind=kLoop, calls=%fused_computation.84.clone.1 | loop fusion | flops 55738368 | bytes 12976512 | tf_op jit(solution)/shard_map/while/body/eval_jaxpr/reduce_sum | solution.py:54
  1511.6 23.7 select_reduce_fusion.11
  1542.4 12.5 dynamic_update_slice.17
  1554.9 12.5 dynamic_update_slice.18
  1575.5 46.7 %select_reduce_fusion.10 = f32[3,384,768]{2,1,0:T(8,128)} fusion(f32[3,32]{1,0:T(4,128)S(1)} %bitcast.251, pred[384,768,32]{1,2,0:T(8,128)(4,1)S(1)} %iota_compare_fusion.8), kind=kLoop, calls=%fused_computation.84.clone.1 | loop fusion | flops 55738368 | bytes 12976512 | tf_op jit(solution)/shard_map/while/body/eval_jaxpr/reduce_sum | solution.py:54
  1630.0 23.7 select_reduce_fusion.11
  1660.8 12.5 dynamic_update_slice.17
  1673.4 12.5 dynamic_update_slice.18
  1694.0 46.7 %select_reduce_fusion.10 = f32[3,384,768]{2,1,0:T(8,128)} fusion(f32[3,32]{1,0:T(4,128)S(1)} %bitcast.251, pred[384,768,32]{1,2,0:T(8,128)(4,1)S(1)} %iota_compare_fusion.8), kind=kLoop, calls=%fused_computation.84.clone.1 | loop fusion | flops 55738368 | bytes 12976512 | tf_op jit(solution)/shard_map/while/body/eval_jaxpr/reduce_sum | solution.py:54
  1748.5 23.7 select_reduce_fusion.11
  1779.3 12.5 dynamic_update_slice.17
  1791.8 12.5 dynamic_update_slice.18
  1812.5 46.7 %select_reduce_fusion.10 = f32[3,384,768]{2,1,0:T(8,128)} fusion(f32[3,32]{1,0:T(4,128)S(1)} %bitcast.251, pred[384,768,32]{1,2,0:T(8,128)(4,1)S(1)} %iota_compare_fusion.8), kind=kLoop, calls=%fused_computation.84.clone.1 | loop fusion | flops 55738368 | bytes 12976512 | tf_op jit(solution)/shard_map/while/body/eval_jaxpr/reduce_sum | solution.py:54
  1867.0 23.7 select_reduce_fusion.11
  1897.8 12.5 dynamic_update_slice.17
  1910.3 12.5 dynamic_update_slice.18
  1930.9 46.7 %select_reduce_fusion.10 = f32[3,384,768]{2,1,0:T(8,128)} fusion(f32[3,32]{1,0:T(4,128)S(1)} %bitcast.251, pred[384,768,32]{1,2,0:T(8,128)(4,1)S(1)} %iota_compare_fusion.8), kind=kLoop, calls=%fused_computation.84.clone.1 | loop fusion | flops 55738368 | bytes 12976512 | tf_op jit(solution)/shard_map/while/body/eval_jaxpr/reduce_sum | solution.py:54
  1985.4 23.7 select_reduce_fusion.11
  2016.2 12.5 dynamic_update_slice.17
  2028.8 12.5 dynamic_update_slice.18
  2049.4 46.7 %select_reduce_fusion.10 = f32[3,384,768]{2,1,0:T(8,128)} fusion(f32[3,32]{1,0:T(4,128)S(1)} %bitcast.251, pred[384,768,32]{1,2,0:T(8,128)(4,1)S(1)} %iota_compare_fusion.8), kind=kLoop, calls=%fused_computation.84.clone.1 | loop fusion | flops 55738368 | bytes 12976512 | tf_op jit(solution)/shard_map/while/body/eval_jaxpr/reduce_sum | solution.py:54
  2103.9 23.7 select_reduce_fusion.11
  2134.7 12.5 dynamic_update_slice.17
  2147.2 12.5 dynamic_update_slice.18
  2167.8 46.7 %select_reduce_fusion.10 = f32[3,384,768]{2,1,0:T(8,128)} fusion(f32[3,32]{1,0:T(4,128)S(1)} %bitcast.251, pred[384,768,32]{1,2,0:T(8,128)(4,1)S(1)} %iota_compare_fusion.8), kind=kLoop, calls=%fused_computation.84.clone.1 | loop fusion | flops 55738368 | bytes 12976512 | tf_op jit(solution)/shard_map/while/body/eval_jaxpr/reduce_sum | solution.py:54
  2222.3 23.7 select_reduce_fusion.11
  2253.1 12.5 dynamic_update_slice.17
  2265.7 12.5 dynamic_update_slice.18
  2307.2 8.4 fusion.147
  2325.9 51.4 %reduce-scatter.17.cloned.1.call-done = f32[384,192]{0,1:T(8,128)} async-done(((f32[6144,192]{0,1:T(8,128)}), f32[384,192]{0,1:T(8,128)}) %reduce-scatter.17.cloned.1.call-update) | async-done | bytes 294928 | tf_op jit(solution)/shard_map/reduce_scatter | solution.py:292
  2379.9 76.3 %reduce-scatter.19.cloned.1.call-done = f32[384,192]{0,1:T(8,128)} async-done(((f32[6144,192]{0,1:T(8,128)}), f32[384,192]{0,1:T(8,128)}) %reduce-scatter.19.cloned.1.call-update) | async-done | bytes 294928 | tf_op jit(solution)/shard_map/reduce_scatter | solution.py:295
  2466.9 33.1 %all-reduce.26.cloned.1.call-done = bf16[384,1472]{0,1:T(8,128)(2,1)} async-done(((bf16[384,1472]{0,1:T(8,128)(2,1)}), bf16[384,1472]{0,1:T(8,128)(2,1)}) %all-reduce.26.cloned.1.call-update) | async-done | bytes 1130512 | tf_op jit(solution)/shard_map/psum | solution.py:305
  2514.2 393.7 %fusion.134 = (f32[96,192]{1,0:T(8,128)S(1)}, f32[96,192]{1,0:T(8,128)S(1)}, f32[96,192]{1,0:T(8,128)S(1)}, f32[96,192]{1,0:T(8,128)S(1)}, f32[96,1792]{1,0:T(8,...) fusion(f32[1472,192]{1,0:T(8,128)S(1)} %copy-done.31, f32[1472,192]{1,0:T(8,128)S(1)} %copy-done.32, ...), kind=kCustom, calls=%all-reduce-scatter.7 | all-reduce-scatter fusion | flops 9437185 | bytes 38535680
  2908.5 28.2 collective-permute-start.3
  2982.1 58.5 %all-reduce.17 = (bf16[6144]{0:T(1024)(128)(2,1)S(1)}, f32[32,3]{0,1:T(4,128)}, f32[1472]{0:T(1024)S(1)}, f32[1472]{0:T(1024)S(1)}, f32[3]{0:T(128)S(1)}) all-reduce(f32[6144]{0:T(1024)S(1)} %reshape.610, f32[32,3]{0,1:T(4,128)} %get-tuple-element.245, ...), channel_id=4, replica_groups=mesh['ctx'=16,'wt'=2] {'ctx'}, use_global_device_ids=true, to_apply=%region_29.31.clone | all-reduce | flops 9187 | bytes 61208
  (830 shorter events, 710.4 us)
Async XLA Ops:
  7.2 1165.4 %copy-start = (bf16[192,1472]{1,0:T(8,128)(2,1)S(1)}, bf16[192,1472]{1,0:T(8,128)(2,1)}, u32[]{:S(2)}) copy-start(bf16[192,1472]{1,0:T(8,128)(2,1)} %param.30) | copy-start | bytes 1695748
  7.2 98.2 %all-gather.4.cloned.1.call-start = ((), (), s32[]{:S(2)}) async-start(), calls=%async_computation.7 | async-start | bytes 2506752 | tf_op jit(solution)/shard_map/all_gather | solution.py:153
  60.4 1154.6 %copy-start.6 = (f32[384,1472]{0,1:T(8,128)}, f32[384,1472]{0,1:T(8,128)S(1)}, u32[]{:S(2)}) copy-start(f32[384,1472]{0,1:T(8,128)S(1)} %copy.130) | copy-start | bytes 6782980
  63.1 85.6 %all-gather.6.cloned.1.call-start = ((), (), s32[]{:S(2)}) async-start(), calls=%async_computation.8 | async-start | bytes 2506752 | tf_op jit(solution)/shard_map/all_gather | solution.py:152
  69.2 9.8 all-to-all-start.1
  72.7 1142.3 %all-reduce.24.cloned.1.call-start = ((), (), s32[]{:S(2)}) async-start(), calls=%async_computation.9 | async-start | bytes 2260992 | tf_op jit(solution)/shard_map/psum | solution.py:209
  1174.3 55.6 %all-to-all-start.3 = ((bf16[16,24,1472]{2,1,0:T(8,128)(2,1)}), bf16[16,24,1472]{2,1,0:T(8,128)(2,1)}, u32[]{:S(2)}, u32[]{:S(2)}) async-start(bf16[16,24,1472]{2,1,0:T(8,128)(2,1)} %bitcast.237), calls=%async_computation.3 | async-start | bytes 2359296 | tf_op jit(solution)/shard_map/all_to_all | solution.py:136
  1178.7 39.0 %copy-start.64 = (f32[1472]{0:T(1024)S(1)}, f32[1472]{0:T(1024)}, u32[]{:S(2)}) copy-start(f32[1472]{0:T(1024)} %param.36) | copy-start | bytes 17668
  1178.7 143.7 %all-reduce.28.cloned.1.call-start = ((), (), s32[]{:S(2)}) async-start(), calls=%async_computation.13 | async-start | bytes 4521984 | tf_op jit(solution)/shard_map/psum | solution.py:224
  1217.6 109.6 %copy-start.68 = (f32[384]{0:T(512)}, f32[384]{0:T(512)S(1)}, u32[]{:S(2)}) copy-start(f32[384]{0:T(512)S(1)} %add_rsqrt_fusion.1) | copy-start | bytes 4612
  1255.6 66.8 %copy-start.9 = (f32[384,1472]{0,1:T(8,128)S(1)}, f32[384,1472]{0,1:T(8,128)}, u32[]{:S(2)}) copy-start(f32[384,1472]{0,1:T(8,128)} %copy-done.8) | copy-start | bytes 6782980
  1255.6 1121.7 %reduce-scatter.17.cloned.1.call-start = ((), (), s32[]{:S(2)}) async-start(), calls=%async_computation.10 | async-start | bytes 5013504 | tf_op jit(solution)/shard_map/reduce_scatter | solution.py:292
  1393.8 23.7 copy-start.2
  1393.8 25.6 copy-start.23
  1423.3 25.7 copy-start.55
  1423.3 25.7 copy-start.59
  1423.3 25.7 copy-start.61
  1511.6 26.3 copy-start.23
  1541.8 25.7 copy-start.55
  1541.8 25.7 copy-start.59
  1541.8 25.7 copy-start.61
  1630.0 23.7 copy-start.2
  1630.0 26.3 copy-start.23
  1660.2 25.7 copy-start.55
  1660.2 25.7 copy-start.59
  1660.2 25.7 copy-start.61
  1748.5 26.3 copy-start.23
  1778.7 25.7 copy-start.55
  1778.7 25.7 copy-start.59
  1778.7 25.7 copy-start.61
  1866.9 26.3 copy-start.23
  1897.1 25.7 copy-start.55
  1897.1 25.7 copy-start.59
  1897.1 25.7 copy-start.61
  1985.4 26.3 copy-start.23
  2015.6 25.7 copy-start.55
  2015.6 25.7 copy-start.59
  2015.6 25.7 copy-start.61
  2103.9 26.3 copy-start.23
  2134.1 25.7 copy-start.55
  2134.1 25.7 copy-start.59
  2134.1 25.7 copy-start.61
  2222.3 26.3 copy-start.23
  2252.5 25.7 copy-start.55
  2252.5 25.7 copy-start.59
  2252.5 25.7 copy-start.61
  2284.7 171.4 %reduce-scatter.19.cloned.1.call-start = ((), (), s32[]{:S(2)}) async-start(), calls=%async_computation.11 | async-start | bytes 5013504 | tf_op jit(solution)/shard_map/reduce_scatter | solution.py:295
  2317.7 190.7 %all-to-all-start.2 = ((bf16[16,24,1472]{2,1,0:T(8,128)(2,1)}), bf16[16,24,1472]{2,1,0:T(8,128)(2,1)}, u32[]{:S(2)}, u32[]{:S(2)}) async-start(bf16[16,24,1472]{2,1,0:T(8,128)(2,1)} %bitcast.7), calls=%async_computation.2 | async-start | bytes 2359296 | tf_op jit(solution)/shard_map/all_to_all | solution.py:326
  2323.5 176.4 %all-reduce.26.cloned.1.call-start = ((), (), s32[]{:S(2)}) async-start(), calls=%async_computation.12 | async-start | bytes 2260992 | tf_op jit(solution)/shard_map/psum | solution.py:305
  2465.2 34.8 %copy-start.7 = (f32[384,1472]{0,1:T(8,128)S(1)}, f32[384,1472]{0,1:T(8,128)}, u32[]{:S(2)}) copy-start(f32[384,1472]{0,1:T(8,128)} %copy-done.6) | copy-start | bytes 6782980
  2465.2 34.8 %copy-start.72 = (f32[384]{0:T(512)S(1)}, f32[384]{0:T(512)}, u32[]{:S(2)}) copy-start(f32[384]{0:T(512)} %copy-done.71) | copy-start | bytes 4612
  2466.9 35.4 %copy-start.27 = (bf16[384,1472]{0,1:T(8,128)(2,1)S(1)}, bf16[384,1472]{0,1:T(8,128)(2,1)}, u32[]{:S(2)}) copy-start(bf16[384,1472]{0,1:T(8,128)(2,1)} %get-tuple-element.814) | copy-start | bytes 3391492
  2466.9 35.4 %copy-start.65 = (f32[1472]{0:T(1024)S(1)}, f32[1472]{0:T(1024)}, u32[]{:S(2)}) copy-start(f32[1472]{0:T(1024)} %param.36) | copy-start | bytes 17668
  2466.9 35.5 %copy-start.69 = (f32[384]{0:T(512)S(1)}, f32[384]{0:T(512)}, u32[]{:S(2)}) copy-start(f32[384]{0:T(512)} %copy-done.68) | copy-start | bytes 4612
  2466.9 35.5 %copy-start.75 = (f32[384]{0:T(512)S(1)}, f32[384]{0:T(512)}, u32[]{:S(2)}) copy-start(f32[384]{0:T(512)} %copy-done.74) | copy-start | bytes 4612
  2508.4 539.4 %all-to-all-start.4 = ((bf16[16,24,1472]{2,1,0:T(8,128)(2,1)}), bf16[16,24,1472]{2,1,0:T(8,128)(2,1)}, u32[]{:S(2)}, u32[]{:S(2)}) async-start(bf16[16,24,1472]{2,1,0:T(8,128)(2,1)} %bitcast.241), calls=%async_computation.6 | async-start | bytes 2359296 | tf_op jit(solution)/shard_map/all_to_all | solution.py:329
  2514.2 429.0 %copy-start.73 = (f32[8,768]{1,0:T(8,128)S(1)}, f32[8,768]{1,0:T(8,128)}, u32[]{:S(2)}) copy-start(f32[8,768]{1,0:T(8,128)} %get-tuple-element.244) | copy-start | bytes 73732
  2908.5 49.5 %collective-permute-start.3 = (f32[60,192]{1,0:T(8,128)S(1)}, f32[60,192]{1,0:T(8,128)S(1)}, u32[]{:S(2)}, u32[]{:S(2)}) collective-permute-start(f32[60,192]{1,0:T(8,128)S(1)} %slice.9), channel_id=1, source_target_pairs={{0,2},{2,4},{4,6},{6,8},{8,10},{10,12},{12,14},{14,16},{16,18},{18... | collective-permute-start | bytes 138248
  2936.8 25.9 collective-permute-start.2
  2948.7 17.0 collective-permute-start.1
  2950.6 15.4 collective-permute-start
  2954.2 14.0 collective-permute-start.6
  2958.0 11.9 collective-permute-start.5
  2962.6 11.9 collective-permute-start.4
  (149 other events, 640.8 us)
Sparse Core Ops, SparseCore 0:
  63.2 42.1 all-gather.3
  108.1 40.5 all-gather.5
  1174.4 40.5 all-reduce.23
  1255.7 66.6 all-reduce.27
  2284.8 92.4 reduce-scatter.16
  2381.5 74.5 reduce-scatter.18
  2459.1 40.8 all-reduce.25
where the time goes:
time: 3070 us; the launch traced here: 3060 us
  other arithmetic  1510 us (49%)
  blocking collectives  512 us (17%)
  local copies, waits for them, and re-layouts  401 us (13%)
  waiting for transfers between devices  312 us (10%)
  matrix products  234 us (8%)
  starting transfers between devices  67 us (2%)
    reduce_sum x24, other arithmetic, pair_terms(): added_terms = jnp.sum(jnp.where(chosen, table_heads, 0.0), axis=-1)  1090 us
    unnamed x2, blocking collectives  452 us
    dynamic_update_slice x40, local copies, waits for them, and re-layouts, local(): lax.scan(partial(backward_step, True), start_state, all_blocks)  228 us
    reduce_sum x8, other arithmetic, table_sums(): summed = jnp.sum(jnp.where(chosen, score_grad[..., None], 0.0), axis=(1, 2))  189 us
    eq x24, other arithmetic, pair_terms(): chosen = bucket[None, :, :, None] == bucket_ids[None, None, None, :]  140 us
    reduce_sum x16, local copies, waits for them, and re-layouts, pair_terms(): added_terms = jnp.sum(jnp.where(chosen, table_heads, 0.0), axis=-1)  82.6 us
    dot_general x24, matrix products, score_block(): jnp.einsum('qhd,khd->hqk', query_heads, key_heads, preferred_element_type...  77.9 us
    reduce_scatter x1, waiting for transfers between devices, local(): lax.psum_scatter(value_parts.reshape(tokens_all, head_cols), 'ctx', scatt...  76.3 us
  transfers between devices with their start and end apart: 18, of which 8 were waited for; matrix products, arithmetic and copies ran while one was open for 17% of the time, Pallas kernels for 0%

commit v1 on v0

v1 whole, which is shorter than its diff:
```python
from functools import partial

import jax
import jax.numpy as jnp
from jax import lax
from jax.experimental import pallas as pl
from jax.experimental.pallas import tpu as pltpu
from jax.sharding import PartitionSpec as P

HD = 64
MIN_LEN = 1024
CHUNK = 128
THRESHOLDS = (1, 2, 3, 4, 5, 6, 7, 8, 12, 16, 23, 32, 46, 64, 91)
MASKED = -1e30
EPSILON = 1e-06
F32 = jnp.float32
BF16 = jnp.bfloat16


def bucket_of(offset):
    distance = jnp.abs(offset)
    bucket_sum = (offset > 0).astype(jnp.int32) * 16
    for threshold in THRESHOLDS:
        bucket_sum = bucket_sum + (distance >= threshold).astype(jnp.int32)
    return bucket_sum


def running_starts(lengths):
    count = lengths.shape[0]
    order = jnp.arange(count, dtype=jnp.int32)
    earlier = order[None, :] < order[:, None]
    return jnp.sum(jnp.where(earlier, lengths[None, :], 0), axis=1)


def places(initial, lengths):
    starts = running_starts(lengths)
    inside = initial[:, None] >= starts[None, :]
    sequence = jnp.sum(inside.astype(jnp.int32), axis=1) - 1
    opening = jnp.max(jnp.where(inside, starts[None, :], 0), axis=1)
    return (sequence, initial - opening)


def dot(left, right):
    return jnp.dot(left, right, preferred_element_type=F32)


def mat_t(left, right):
    return lax.dot_general(left, right, (((1,), (1,)), ((), ())), preferred_element_type=F32)


def t_mat(left, right):
    return lax.dot_general(left, right, (((0,), (0,)), ((), ())), preferred_element_type=F32)


def norm_back(grad_in, normed, inverse, gain_in):
    scaled = grad_in * gain_in
    return inverse * (scaled - normed * jnp.mean(scaled * normed, axis=-1, keepdims=True))


def pair_terms(table_here, query_seq, query_pos, key_seq, key_pos, key_mask):
    bucket = bucket_of(key_pos[None, :] - query_pos[:, None])
    bucket_ids = jnp.arange(table_here.shape[0], dtype=jnp.int32)
    chosen = bucket[None, :, :, None] == bucket_ids[None, None, None, :]
    table_heads = jnp.transpose(table_here)[:, None, None, :]
    added_terms = jnp.sum(jnp.where(chosen, table_heads, 0.0), axis=-1)
    added_terms = added_terms + key_mask.astype(F32)[None, None, :]
    same_seq = key_seq[None, :] == query_seq[:, None]
    return (added_terms, same_seq, chosen)


def score_block(query_heads, key_heads, added_terms, same_seq):
    raw_score = jnp.einsum("qhd,khd->hqk", query_heads, key_heads, preferred_element_type=F32)
    return jnp.where(same_seq[None], raw_score + added_terms, MASKED)


class General:
    def __init__(self, q, k, v, mask, lengths, table):
        self.tok = q.shape[0]
        self.cols = q.shape[1]
        heads = self.cols // HD
        self.table = table
        n = lax.axis_size("ctx")
        self.all = self.tok * n
        rows = 2 * self.tok
        blocks = self.all // rows
        seq_all, pos_all = places(jnp.arange(self.all, dtype=jnp.int32), lengths)
        first = lax.axis_index("ctx") * self.tok
        self.q_seq = lax.dynamic_slice_in_dim(seq_all, first, self.tok)
        self.q_pos = lax.dynamic_slice_in_dim(pos_all, first, self.tok)
        self.q = q.reshape(self.tok, heads, HD)
        self.blocks = (
            lax.all_gather(k, "ctx", axis=0, tiled=True).reshape(blocks, rows, heads, HD),
            lax.all_gather(v, "ctx", axis=0, tiled=True).reshape(blocks, rows, heads, HD),
            seq_all.reshape(blocks, rows),
            pos_all.reshape(blocks, rows),
            lax.all_gather(mask, "ctx", axis=0, tiled=True).reshape(blocks, rows),
        )
        self.heads = heads

    def forward(self):
        def top_step(state, block):
            top, total = state
            k, _, seq, pos, mask = block
            added, same, _ = pair_terms(self.table, self.q_seq, self.q_pos, seq, pos, mask)
            scores = score_block(self.q, k, added, same)
            new_top = jnp.maximum(top, jnp.max(scores, axis=-1))
            total = total * jnp.exp(top - new_top) + jnp.sum(
                jnp.exp(scores - new_top[..., None]), axis=-1
            )
            return ((new_top, total), None)

        def value_step(out, block):
            high, low = out
            k, v, seq, pos, mask = block
            added, same, _ = pair_terms(self.table, self.q_seq, self.q_pos, seq, pos, mask)
            probs = jnp.exp(score_block(self.q, k, added, same) - self.lse[..., None])
            probs_high = probs.astype(BF16)
            rest = (probs - probs_high.astype(F32)).astype(BF16)
            high = high + jnp.einsum("hqk,khd->qhd", probs_high, v, preferred_element_type=F32)
            low = low + jnp.einsum("hqk,khd->qhd", rest, v, preferred_element_type=F32)
            return ((high, low), None)

        start = (
            jnp.full((self.heads, self.tok), MASKED, F32),
            jnp.zeros((self.heads, self.tok), F32),
        )
        (top, total), _ = lax.scan(top_step, start, self.blocks)
        self.lse = top + jnp.log(total)
        self.zero = jnp.zeros((self.tok, self.heads, HD), F32)
        (high, low), _ = lax.scan(value_step, (self.zero, self.zero), self.blocks)
        self.exact = high + low
        return high.reshape(self.tok, self.cols).astype(BF16)

    def backward(self, do):
        grad = do.reshape(self.tok, self.heads, HD)
        delta = jnp.transpose(jnp.sum(grad.astype(F32) * self.exact, axis=-1))

        def step(state, block):
            q_acc, table_acc = state
            k, v, seq, pos, mask = block
            added, same, chosen = pair_terms(self.table, self.q_seq, self.q_pos, seq, pos, mask)
            probs = jnp.exp(score_block(self.q, k, added, same) - self.lse[..., None])
            dp = jnp.einsum("qhd,khd->hqk", grad, v, preferred_element_type=F32)
            ds = probs * (dp - delta[..., None])
            low = ds.astype(BF16)
            q_acc = q_acc + jnp.einsum("hqk,khd->qhd", low, k, preferred_element_type=F32)
            sums = jnp.sum(jnp.where(chosen, ds[..., None], 0.0), axis=(1, 2))
            emitted = (
                jnp.einsum("hqk,qhd->khd", low, self.q, preferred_element_type=F32),
                jnp.einsum("hqk,qhd->khd", probs.astype(BF16), grad, preferred_element_type=F32),
                jnp.sum(ds, axis=(0, 1)),
            )
            return ((q_acc, table_acc + jnp.transpose(sums)), emitted)

        start = (self.zero, jnp.zeros((self.table.shape[0], self.heads), F32))
        (q_acc, table_acc), (dk, dv, dm) = lax.scan(step, start, self.blocks)
        dk = lax.psum_scatter(
            dk.reshape(self.all, self.cols), "ctx", scatter_dimension=0, tiled=True
        )
        dv = lax.psum_scatter(
            dv.reshape(self.all, self.cols), "ctx", scatter_dimension=0, tiled=True
        )
        dq = q_acc.reshape(self.tok, self.cols)
        return (dq.astype(BF16), dk.astype(BF16), dv.astype(BF16), table_acc, dm.reshape(self.all))


def head_lanes(shape, head, value_order):
    lane = lax.broadcasted_iota(jnp.int32, shape, 1) // HD
    place = (head + 2 if head < 2 else 1) if value_order else head
    return lane == place


def chunk_place(ctx, i, chunks, halo):
    g = ctx * chunks + i
    per = MIN_LEN // CHUNK
    within = lax.rem(g, per)
    window = (g - within) * CHUNK - (ctx - halo) * chunks * CHUNK
    return within, pl.multiple_of(window, CHUNK)


def bias_fill(near_ref, bias_ref, heads):
    per = MIN_LEN // CHUNK
    for h in range(heads):
        strip = near_ref[h : h + 1, :]
        wide = jnp.broadcast_to(strip, (CHUNK, 512))
        tile = pltpu.roll(wide, 512 - 127, 1, stride=1, stride_axis=0)
        bias_ref[h, :, pl.ds(0, (per - 2) * CHUNK)] = jnp.broadcast_to(
            strip[:, 0:1], (CHUNK, (per - 2) * CHUNK)
        )
        bias_ref[h, :, pl.ds((per - 2) * CHUNK, 3 * CHUNK)] = tile[:, : 3 * CHUNK]
        bias_ref[h, :, pl.ds((per + 1) * CHUNK, (per - 2) * CHUNK)] = jnp.broadcast_to(
            strip[:, 510:511], (CHUNK, (per - 2) * CHUNK)
        )


def forward_kernel(halo, heads, q_ref, kv_ref, mask_ref, near_ref, o_ref, lse_ref, bias_ref):
    ctx = lax.axis_index("ctx")
    chunks = q_ref.shape[0] // CHUNK
    per = MIN_LEN // CHUNK
    bias_fill(near_ref, bias_ref, heads)
    for i in range(chunks):
        within, window = chunk_place(ctx, i, chunks, halo)
        q = q_ref[i * CHUNK : (i + 1) * CHUNK, :]
        keys = kv_ref[pl.ds(window, MIN_LEN), 0:256]
        values = kv_ref[pl.ds(window, MIN_LEN), 128:384]
        mask = mask_ref[:, pl.ds(window, MIN_LEN)]
        out = jnp.zeros((CHUNK, 256), F32)
        lse = jnp.zeros((CHUNK, CHUNK), F32)
        for h in range(heads):
            s = mat_t(jnp.where(head_lanes(q.shape, h, False), q, jnp.zeros_like(q)), keys)
            start = pl.multiple_of((per - 1 - within) * CHUNK, CHUNK)
            s = s + bias_ref[h, :, pl.ds(start, MIN_LEN)] + mask
            top = jnp.max(s, axis=1, keepdims=True)
            e = jnp.exp(s - top)
            total = jnp.sum(e, axis=1, keepdims=True)
            p = (e * (1.0 / total)).astype(BF16)
            out = jnp.where(head_lanes(out.shape, h, True), dot(p, values), out)
            lane = lax.broadcasted_iota(jnp.int32, lse.shape, 1)
            lse = jnp.where(lane == h, top + jnp.log(total), lse)
        o_ref[i * CHUNK : (i + 1) * CHUNK, :] = out.astype(BF16)
        lse_ref[i * CHUNK : (i + 1) * CHUNK, :] = lse


def fold_diagonals(tile):
    rows = tile.shape[0]
    width = tile.shape[1]
    while rows > 1:
        rows //= 2
        tile = tile[:rows] + pltpu.roll(tile[rows:], width - rows, 1)
    return tile


def backward_kernel(
    halo,
    heads,
    q_ref,
    kv_ref,
    mask_ref,
    near_ref,
    do_ref,
    lse_ref,
    dq_ref,
    dkv_ref,
    dmask_ref,
    dnear_ref,
    dfar_ref,
    bias_ref,
    acc_ref,
    ds_ref,
    tile_ref,
):
    ctx = lax.axis_index("ctx")
    chunks = q_ref.shape[0] // CHUNK
    per = MIN_LEN // CHUNK
    bias_fill(near_ref, bias_ref, heads)
    acc_ref[...] = jnp.zeros_like(acc_ref)
    dmask_ref[...] = jnp.zeros_like(dmask_ref)
    tile_ref[...] = jnp.zeros_like(tile_ref)
    ds_ref[:, 0:CHUNK] = jnp.zeros((CHUNK, CHUNK), F32)
    ds_ref[:, MIN_LEN + CHUNK :] = jnp.zeros((CHUNK, CHUNK), F32)
    far = [jnp.zeros((1, MIN_LEN), F32) for _ in range(2 * heads)]
    for i in range(chunks):
        within, window = chunk_place(ctx, i, chunks, halo)
        rows = slice(i * CHUNK, (i + 1) * CHUNK)
        q = q_ref[rows, :]
        do = do_ref[rows, :]
        lse = lse_ref[rows, :]
        keys = kv_ref[pl.ds(window, MIN_LEN), 0:256]
        values = kv_ref[pl.ds(window, MIN_LEN), 128:384]
        mask = mask_ref[:, pl.ds(window, MIN_LEN)]
        column = lax.broadcasted_iota(jnp.int32, (1, MIN_LEN), 1) // CHUNK
        dq = jnp.zeros((CHUNK, 256), F32)
        dmask = jnp.zeros((1, MIN_LEN), F32)
        dkeys = jnp.zeros((MIN_LEN, 256), F32)
        dvalues = jnp.zeros((MIN_LEN, 256), F32)
        for h in range(heads):
            qm = jnp.where(head_lanes(q.shape, h, False), q, jnp.zeros_like(q))
            dom = jnp.where(head_lanes(do.shape, h, True), do, jnp.zeros_like(do))
            start = pl.multiple_of((per - 1 - within) * CHUNK, CHUNK)
            s = mat_t(qm, keys) + bias_ref[h, :, pl.ds(start, MIN_LEN)] + mask
            p = jnp.exp(s - lse[:, h : h + 1])
            dp = mat_t(dom, values)
            delta = jnp.sum(p * dp, axis=1, keepdims=True)
            ds = p * (dp - delta)
            low = ds.astype(BF16)
            dq = jnp.where(head_lanes(dq.shape, h, False), dot(low, keys), dq)
            dkeys = dkeys + t_mat(low, qm)
            dvalues = dvalues + t_mat(p.astype(BF16), dom)
            sums = jnp.sum(ds, axis=0, keepdims=True)
            dmask = dmask + sums
            far[2 * h] = far[2 * h] + jnp.where(column < within - 1, sums, 0.0)
            far[2 * h + 1] = far[2 * h + 1] + jnp.where(column > within + 1, sums, 0.0)
            ds_ref[:, CHUNK : CHUNK + MIN_LEN] = ds
            near = pl.multiple_of(within * CHUNK, CHUNK)
            tile_ref[h, :, 0 : 3 * CHUNK] += ds_ref[:, pl.ds(near, 3 * CHUNK)]
        dq_ref[rows, :] = dq.astype(BF16)
        dmask_ref[:, pl.ds(window, MIN_LEN)] += dmask
        acc_ref[pl.ds(window, MIN_LEN), 0:256] += dkeys
        acc_ref[pl.ds(window, MIN_LEN), 128:384] += dvalues
    dkv_ref[...] = acc_ref[...].astype(BF16)
    for h in range(heads):
        dnear_ref[h : h + 1, :] = fold_diagonals(tile_ref[h])
        for side in range(2):
            dfar_ref[2 * h + side : 2 * h + side + 1, :] = jnp.broadcast_to(
                jnp.sum(far[2 * h + side], axis=1, keepdims=True), (1, CHUNK)
            )


def needed_blocks(ctx, tok):
    low = (ctx * tok) // MIN_LEN * MIN_LEN
    high = ((ctx + 1) * tok + MIN_LEN - 1) // MIN_LEN * MIN_LEN
    return low // tok, -(-high // tok)


def whole_spec():
    return pl.BlockSpec(memory_space=pltpu.VMEM)


class Even:
    def __init__(self, q, kv, mask, table):
        self.tok = q.shape[0]
        self.heads = table.shape[1]
        n = lax.axis_size("ctx")
        self.count = n
        self.ctx = lax.axis_index("ctx")
        spans = [needed_blocks(c, self.tok) for c in range(n)]
        self.shifts = sorted(
            {j - c for c in range(n) for j in range(max(spans[c][0], 0), min(spans[c][1], n))}
            - {0},
            key=abs,
        )
        self.pairs = {
            s: [(c + s, c) for c in range(n) if spans[c][0] <= c + s < min(spans[c][1], n)]
            for s in self.shifts
        }
        self.halo = max(abs(s) for s in self.shifts)
        self.q = q
        blocks = {0: kv}
        for s in self.shifts:
            blocks[s] = lax.ppermute(kv, "ctx", self.pairs[s])
        zero = jnp.zeros_like(kv)
        self.kv = jnp.concatenate(
            [blocks.get(s, zero) for s in range(-self.halo, self.halo + 1)], axis=0
        )
        pad = self.halo * self.tok
        padded = jnp.pad(lax.all_gather(mask, "ctx", axis=0, tiled=True).astype(F32), (pad, pad))
        self.window = (2 * self.halo + 1) * self.tok
        self.mask = lax.dynamic_slice_in_dim(padded, self.ctx * self.tok, self.window)[None, :]
        offsets = jnp.arange(512, dtype=jnp.int32) - 255
        ids = jnp.arange(table.shape[0], dtype=jnp.int32)
        self.chosen = bucket_of(offsets)[:, None] == ids[None, :]
        self.near = jnp.sum(jnp.where(self.chosen[None], jnp.transpose(table)[:, None, :], 0.0), -1)

    def forward(self):
        o, self.lse = pl.pallas_call(
            partial(forward_kernel, self.halo, self.heads),
            out_shape=(
                jax.ShapeDtypeStruct((self.tok, 256), BF16),
                jax.ShapeDtypeStruct((self.tok, CHUNK), F32),
            ),
            in_specs=[whole_spec()] * 4,
            out_specs=(whole_spec(), whole_spec()),
            scratch_shapes=[pltpu.VMEM((self.heads, CHUNK, 2 * MIN_LEN - CHUNK), F32)],
            compiler_params=pltpu.CompilerParams(vmem_limit_bytes=40 << 20),
            name="attend",
        )(self.q, self.kv, self.mask, self.near)
        return jnp.concatenate([o[:, 128:], o[:, 64:128]], axis=1)

    def backward(self, do):
        spread = jnp.concatenate([jnp.zeros((self.tok, 64), BF16), do[:, 128:], do[:, :128]], 1)
        dq, dkv, dmask, dnear, dfar = pl.pallas_call(
            partial(backward_kernel, self.halo, self.heads),
            out_shape=(
                jax.ShapeDtypeStruct((self.tok, 256), BF16),
                jax.ShapeDtypeStruct((self.window, 384), BF16),
                jax.ShapeDtypeStruct((1, self.window), F32),
                jax.ShapeDtypeStruct((self.heads, 512), F32),
                jax.ShapeDtypeStruct((2 * self.heads, CHUNK), F32),
            ),
            in_specs=[whole_spec()] * 6,
            out_specs=(whole_spec(),) * 5,
            scratch_shapes=[
                pltpu.VMEM((self.heads, CHUNK, 2 * MIN_LEN - CHUNK), F32),
                pltpu.VMEM((self.window, 384), F32),
                pltpu.VMEM((CHUNK, MIN_LEN + 2 * CHUNK), F32),
                pltpu.VMEM((self.heads, CHUNK, 512), F32),
            ],
            compiler_params=pltpu.CompilerParams(vmem_limit_bytes=40 << 20),
            name="attend_back",
        )(self.q, self.kv, self.mask, self.near, spread, self.lse)
        tok = self.tok
        total = dkv[self.halo * tok : (self.halo + 1) * tok].astype(F32)
        for s in self.shifts:
            part = dkv[(self.halo + s) * tok : (self.halo + s + 1) * tok]
            back = lax.ppermute(part, "ctx", [(b, a) for a, b in self.pairs[s]])
            total = total + back.astype(F32)
        total = total.astype(BF16)
        dk = total[:, :192]
        dv = jnp.concatenate([total[:, 256:], total[:, 192:256]], axis=1)
        offsets = jnp.arange(512, dtype=jnp.int32)
        offsets = jnp.where(offsets < 3 * CHUNK, offsets, offsets - 512) - CHUNK
        ids = jnp.arange(self.chosen.shape[1], dtype=jnp.int32)
        chosen = bucket_of(offsets)[:, None] == ids[None, :]
        table = jnp.sum(jnp.where(chosen[None], dnear[:, :, None], 0.0), axis=1)
        table = table + jnp.where(ids == 15, 1.0, 0.0)[None] * dfar[0::2, :1]
        table = table + jnp.where(ids == 31, 1.0, 0.0)[None] * dfar[1::2, :1]
        pad = self.halo * tok
        spread_mask = lax.dynamic_update_slice_in_dim(
            jnp.zeros((self.count * tok + 2 * pad,), F32), dmask[0], self.ctx * tok, 0
        )
        return dq[:, :192], dk, dv, jnp.transpose(table), spread_mask[pad : pad + self.count * tok]


class Halving:
    def __init__(self, width):
        self.n = lax.axis_size("ctx")
        self.bits = self.n.bit_length() - 1
        self.own = width // self.n
        self.rows = -(-self.own // 16) * 16
        places = [int(format(b, f"0{self.bits}b")[::-1], 2) for b in range(self.n)]
        order = jnp.asarray(places, jnp.int32)
        owner = jnp.bitwise_xor(order, lax.axis_index("ctx"))
        inner = jnp.arange(self.rows, dtype=jnp.int32)
        source = jnp.where(inner < self.own, owner[:, None] * self.own + inner, -1).reshape(-1)
        features = jnp.arange(width, dtype=jnp.int32)
        self.select = (features[:, None] == source[None, :]).astype(BF16)

    def arrange(self, x):
        return dot(x, self.select).astype(BF16)

    def scatter(self, left, right):
        half = left.shape[1] // 2
        send = t_mat(left[:, half:], right).astype(BF16)
        keep = t_mat(left[:, :half], right).astype(BF16)
        for bit in range(self.bits):
            pairs = [(i, i ^ (1 << bit)) for i in range(self.n)]
            got = lax.ppermute(send, "ctx", pairs)
            half = half // 2
            if bit == self.bits - 1:
                return keep[: self.own].astype(F32) + got[: self.own].astype(F32)
            send = (keep[half:].astype(F32) + got[half:].astype(F32)).astype(BF16)
            keep = (keep[:half].astype(F32) + got[:half].astype(F32)).astype(BF16)


def local(
    inputs,
    delete_mask,
    lengths,
    dealing,
    w_query,
    w_key,
    w_value,
    w_output,
    bias_table,
    norm_attn,
    w_gate,
    w_up,
    w_down,
    norm_ffn,
    out_grad,
):
    tok = inputs.shape[0]
    width = inputs.shape[1]
    n = lax.axis_size("ctx")
    ctx = lax.axis_index("ctx")
    wt = lax.axis_index("wt")
    tokens_all = tok * n
    cols = w_query.shape[1]
    even = (
        tokens_all == MIN_LEN * lengths.shape[0]
        and tok % CHUNK == 0
        and cols == 3 * HD
        and lax.axis_size("wt") == 2
    )
    swap = [(0, 1), (1, 0)]

    def other(x):
        return lax.ppermute(x, "wt", swap)

    sums = Halving(width)
    stream_in = inputs.astype(F32)
    inverse_one = lax.rsqrt(jnp.mean(stream_in * stream_in, axis=-1, keepdims=True) + EPSILON)
    normed_one = stream_in * inverse_one
    hidden_one = (normed_one * norm_attn).astype(BF16)
    if even:
        joined = jnp.concatenate([w_key, w_value[:, 128:], w_value[:, :128]], axis=1)
        queries = dot(hidden_one, jnp.pad(w_query, ((0, 0), (0, 64)))).astype(BF16)
        attention = Even(queries, dot(hidden_one, joined).astype(BF16), delete_mask, bias_table)
    else:
        attention = General(
            dot(hidden_one, w_query).astype(BF16),
            dot(hidden_one, w_key).astype(BF16),
            dot(hidden_one, w_value).astype(BF16),
            delete_mask,
            lengths,
            bias_table,
        )
    w_output_other = other(w_output)
    arranged_grad = sums.arrange(out_grad)
    arranged_one = sums.arrange(hidden_one)
    inner_grad = mat_t(out_grad, w_down)
    attended = attention.forward()
    branch_attn = dot(attended, w_output) + dot(other(attended), w_output_other)
    stream_mid = stream_in + branch_attn
    inverse_two = lax.rsqrt(jnp.mean(stream_mid * stream_mid, axis=-1, keepdims=True) + EPSILON)
    normed_two = stream_mid * inverse_two
    hidden_two = (normed_two * norm_ffn).astype(BF16)
    gate_value = dot(hidden_two, w_gate)
    up_value = dot(hidden_two, w_up)

    def gated_unit(gate_in, up_in):
        return jax.nn.gelu(gate_in, approximate=True) * up_in

    activated, gated_pull = jax.vjp(gated_unit, gate_value, up_value)
    inner_low = activated.astype(BF16)
    down_part = sums.scatter(arranged_grad, inner_low)
    gate_grad, up_grad = gated_pull(inner_grad)
    gate_low = gate_grad.astype(BF16)
    up_low = up_grad.astype(BF16)
    back_part = (mat_t(gate_low, w_gate) + mat_t(up_low, w_up)).astype(BF16)
    hidden_two_grad = back_part.astype(F32) + other(back_part).astype(F32)
    arranged_two = sums.arrange(hidden_two)
    gate_part = sums.scatter(arranged_two, gate_low)
    up_part = sums.scatter(arranged_two, up_low)
    gain_two_grad = jnp.sum(hidden_two_grad * normed_two, axis=0)
    stream_mid_grad = out_grad.astype(F32) + norm_back(
        hidden_two_grad, normed_two, inverse_two, norm_ffn
    )
    attn_grad_low = stream_mid_grad.astype(BF16)
    attended_grad = mat_t(attn_grad_low, w_output).astype(BF16)
    output_part = sums.scatter(sums.arrange(attn_grad_low), attended)
    ffn_part = dot(inner_low, w_down).astype(BF16)
    branch_ffn = ffn_part.astype(F32) + other(ffn_part).astype(F32)
    stream_out = stream_mid + branch_ffn
    squares = jnp.stack(
        [
            jnp.sum(stream_out * stream_out),
            jnp.sum(branch_attn * branch_attn),
            jnp.sum(branch_ffn * branch_ffn),
        ]
    )
    dq, dk, dv, table_acc, dmask = attention.backward(attended_grad)
    projections = jnp.concatenate([dq, dk, dv], axis=1)
    projection_part = sums.scatter(arranged_one, projections)
    w_all = jnp.concatenate([w_query, w_key, w_value], axis=1)
    one_part = mat_t(projections, w_all).astype(BF16)
    hidden_one_grad = one_part.astype(F32) + other(one_part).astype(F32)
    gain_one_grad = jnp.sum(hidden_one_grad * normed_one, axis=0)
    input_grad = stream_mid_grad + norm_back(hidden_one_grad, normed_one, inverse_one, norm_attn)
    heads = table_acc.shape[1]
    flat = table_acc.reshape(-1)
    table_slots = jnp.where(
        jnp.arange(2)[:, None] == wt, jnp.broadcast_to(flat, (2, flat.shape[0])), 0.0
    ).reshape(-1)
    small = jnp.concatenate(
        [
            dmask,
            table_slots,
            0.5 * gain_one_grad,
            0.5 * gain_two_grad,
            0.5 * squares,
        ]
    )
    small = lax.psum(small, ("ctx", "wt"))
    mask_all = small[:tokens_all].reshape(n, 1, tok)
    base = tokens_all
    table_grad = lax.dynamic_slice_in_dim(small, base + wt * flat.shape[0], flat.shape[0])
    table_grad = table_grad.reshape(-1, heads)
    base += 2 * flat.shape[0]
    own = width // n
    gain_one = lax.dynamic_slice_in_dim(small, base + ctx * own, own)
    gain_two = lax.dynamic_slice_in_dim(small, base + width + ctx * own, own)
    square_sum = small[base + 2 * width :]
    root_means = jnp.sqrt(square_sum / (tokens_all * width))
    quota = tok // n
    slots = lax.dynamic_slice_in_dim(dealing, ctx * tok, tok).reshape(n, quota, 1)
    inside = slots - (jnp.arange(n, dtype=jnp.int32) * tok)[:, None, None]
    chosen = inside == jnp.arange(tok, dtype=jnp.int32)[None, None, :]
    mask_grad = jnp.sum(jnp.where(chosen, mask_all, 0.0), axis=-1).reshape(tok)
    return (
        stream_out.astype(BF16),
        input_grad.astype(BF16),
        mask_grad.astype(BF16),
        projection_part[:, :cols],
        projection_part[:, cols : 2 * cols],
        projection_part[:, 2 * cols :],
        jnp.transpose(output_part),
        table_grad,
        gain_one,
        gate_part,
        up_part,
        jnp.transpose(down_part),
        gain_two,
        root_means,
    )


def solution(mesh):
    return jax.shard_map(
        local,
        mesh=mesh,
        in_specs=(
            P("ctx", None),
            P("ctx"),
            P(),
            P(),
            P(None, "wt"),
            P(None, "wt"),
            P(None, "wt"),
            P("wt", None),
            P(None, "wt"),
            P(),
            P(None, "wt"),
            P(None, "wt"),
            P("wt", None),
            P(),
            P("ctx", None),
        ),
        out_specs=(
            P("ctx", None),
            P("ctx", None),
            P("ctx"),
            P("ctx", "wt"),
            P("ctx", "wt"),
            P("ctx", "wt"),
            P("wt", "ctx"),
            P(None, "wt"),
            P("ctx"),
            P("ctx", "wt"),
            P("ctx", "wt"),
            P("wt", "ctx"),
            P("ctx"),
            P(),
        ),
        check_vma=False,
    )
```

time: 3070 us -> 433 us (0.14)
  other arithmetic: 1510 us -> 41.3 us
  blocking collectives: 512 us -> 63.9 us
  local copies, waits for them, and re-layouts: 401 us -> 15.6 us
  matrix products: 234 us -> 64.6 us
  waiting for transfers between devices: 312 us -> 160 us
    reduce_sum x43 -> x4, other arithmetic: 1290 us -> 3.83 us  [the longest x1 3.39 us: local(): jnp.sum(stream_out * stream_out)]
    unnamed x2 -> x0, blocking collectives: 452 us -> none
    dynamic_update_slice x40 -> x1, local copies, waits for them, and re-layouts: 228 us -> 0.34 us  [backward(): lax.dynamic_update_slice_in_dim(jnp.zeros((self.count * tok + 2 * pad,),...]
    dot_general x93 -> x26, matrix products: 234 us -> 64.6 us  [the longest x11 27.6 us: dot(): return jnp.dot(left, right, preferred_element_type=F32)]
    ppermute x0 -> x37, waiting for transfers between devices: none -> 160 us  [the longest x20 114 us: scatter(): got = lax.ppermute(send, 'ctx', pairs)]
    eq x48 -> x3, other arithmetic: 145 us -> 0.54 us  [the longest x1 0.51 us: local(): jnp.arange(2)[:, None] == wt]
    psum x3 -> x0, waiting for transfers between devices: 133 us -> none  [the longest x1 64.2 us: local(): lax.psum(jnp.dot(inner_low, w_down, preferred_element_type=jnp.float32).a...]
    reduce_scatter x2 -> x0, waiting for transfers between devices: 128 us -> none  [the longest x1 76.3 us: local(): lax.psum_scatter(value_parts.reshape(tokens_all, head_cols), 'ctx', scatt...]
  transfers between devices with their start and end apart: 18 -> 37, of which waited for: 8 -> 15; matrix products, arithmetic and copies ran while one was open for 17% -> 18% of each run, Pallas kernels for 0% -> 1%
where the time goes in v1:
time: 433 us; the launch traced here: 426 us
  waiting for transfers between devices  160 us (37%)
  matrix products  64.6 us (15%)
  blocking collectives  63.9 us (15%)
  starting transfers between devices  63.7 us (15%)
  other arithmetic  41.3 us (10%)
  local copies, waits for them, and re-layouts  15.6 us (4%)
  Pallas kernels  14.3 us (3%)
    ppermute x20, waiting for transfers between devices, scatter(): got = lax.ppermute(send, 'ctx', pairs)  114 us
    ppermute x5, waiting for transfers between devices, other(): return lax.ppermute(x, 'wt', swap)  46.2 us
    psum x1, blocking collectives, local(): small = lax.psum(small, ('ctx', 'wt'))  41.5 us
    dot_general x11, matrix products, dot(): return jnp.dot(left, right, preferred_element_type=F32)  27.6 us
    ppermute x20, starting transfers between devices, scatter(): got = lax.ppermute(send, 'ctx', pairs)  25.4 us
    dot_general x10, matrix products, t_mat(): lax.dot_general(left, right, (((0,), (0,)), ((), ())), preferred_element_...  24.6 us
    all_gather x1, blocking collectives, __init__(): lax.all_gather(mask, 'ctx', axis=0, tiled=True).astype(F32)  22.3 us
    convert_element_type x10, other arithmetic, scatter(): keep = (keep[:half].astype(F32) + got[:half].astype(F32)).astype(BF16)  19.9 us
  transfers between devices with their start and end apart: 37, of which 15 were waited for; matrix products, arithmetic and copies ran while one was open for 18% of the time, Pallas kernels for 1%

profile of v1, /device:TPU:0, one launch (start us, length us, event | category | flops | bytes accessed | tf_op | source)
XLA Modules:
  0.0 425.8 jit_solution(16441360940901633994)
XLA Ops:
  0.7 1.7 fusion.32
  2.5 2.3 convolution_convert_fusion.12
  6.2 7.8 %collective-permute-start.1 = (bf16[384,384]{1,0:T(8,128)(2,1)S(1)}, bf16[384,384]{1,0:T(8,128)(2,1)}, u32[]{:S(2)}, u32[]{:S(2)}) collective-permute-start(bf16[384,384]{1,0:T(8,128)(2,1)S(1)} %convolution_convert_fusion.12), channel_id=1, source_target_pairs={{0,4},{4,8},{6,10},{10,14},{16,20},{20,24},{22,26},{26,30},{1,5},{... | collective-permute-start | bytes 884744 | tf_op jit(solution)/shard_map/ppermute | solution.py:340
  14.0 2.0 collective-permute-start.2
  19.5 22.3 %all-gather = bf16[16,1,384]{2,1,0:T(2,128)(2,1)S(1)} all-gather(bf16[1,1,384]{2,1,0:T(2,128)(2,1)S(1)} %reshape.291), channel_id=1, replica_groups=mesh['ctx'=16,'wt'=2] {'ctx'}, dimensions={0}, use_global_device_ids=true | all-gather | bytes 13056 | tf_op jit(solution)/shard_map/all_gather | solution.py:346
  43.0 3.3 fusion.13
  46.3 3.8 fusion.24
  53.4 1.5 collective-permute-start.7
  59.1 5.1 %attend.1 = (bf16[384,256]{1,0:T(8,128)(2,1)S(1)}, f32[384,128]{1,0:T(8,128)S(1)}) custom-call(bf16[384,256]{1,0:T(8,128)(2,1)S(1)} %convolution_convert_fusion.13.q_ref, bf16[2688,384]{1,0:T(8,128)(2,1)S(1)} %constant_dynamic-update-slice_fusion.kv_ref, f32[1,2688]{1,0:T(1,128)S(1)} %broadcast_in_dim.118.mask_ref, f32[3,512]{1,0:T(4,128)S(1)} %select_reduce_fusion.2.near_ref), custom_call_target="tpu_custom_call" | custom-call | tf_op jit(solution)/shard_map/attend/pallas_call | solution.py:355
  65.6 7.6 %collective-permute-done.6 = bf16[384,192]{1,0:T(8,128)(2,1)S(1)} collective-permute-done((bf16[384,192]{1,0:T(8,128)(2,1)S(1)}, bf16[384,192]{1,0:T(8,128)(2,1)S(1)}, u32[]{:S(2)}, u32[]{:S(2)}) %collective-permute-start.6) | collective-permute-done | bytes 147488 | tf_op jit(solution)/shard_map/ppermute | solution.py:478
  73.2 1.6 multiply_reduce_fusion.5
  75.2 2.2 fusion.15
  78.6 2.4 fusion.93
  81.0 2.9 fusion.94
  83.9 4.7 %multiply_convert_fusion = (bf16[384,1792]{1,0:T(8,128)(2,1)S(1)}, bf16[384,1792]{1,0:T(8,128)(2,1)S(1)}, bf16[384,1792]{1,0:T(8,128)(2,1)S(1)}) fusion(f32[384,1792]{1,0:T(8,128)S(1)} %fusion.93, f32[384,1792]{1,0:T(8,128)S(1)} %fusion.94, bf16[384,1472]{0,1:T(8,128)(2,1)S(1)} %copy-done.10, bf16[1792,1472]{0,1:T(8,128)(2,1)S(1)} %bitcast.48), kind=kOutput, calls=%fused_computation.46 | convolution fusion | flops 2043740160 | bytes 16039936 | tf_op jit(solution)/shard_map/dot_general | solution.py:48
  88.6 2.9 fusion.95
  91.6 3.1 convolution_convert_fusion.4
  94.7 3.2 convolution_convert_fusion.5
  97.9 2.9 convolution_convert_fusion.7
  100.9 1.6 collective-permute-start.8
  102.4 3.0 fusion.12
  106.0 3.2 convolution_convert_fusion.2
  109.2 3.3 convolution_convert_fusion.3
  112.5 3.1 convolution_convert_fusion
  115.6 3.1 convolution_convert_fusion.1
  118.8 10.0 %collective-permute-done.8 = bf16[384,1472]{0,1:T(8,128)(2,1)S(1)} collective-permute-done((bf16[384,1472]{0,1:T(8,128)(2,1)S(1)}, bf16[384,1472]{0,1:T(8,128)(2,1)S(1)}, u32[]{:S(2)}, u32[]{:S(2)}) %collective-permute-start.8) | collective-permute-done | bytes 1130528 | tf_op jit(solution)/shard_map/ppermute | solution.py:478
  128.8 22.7 %collective-permute-done.9 = bf16[384,1472]{0,1:T(8,128)(2,1)S(1)} collective-permute-done((bf16[384,1472]{0,1:T(8,128)(2,1)S(1)}, bf16[384,1472]{0,1:T(8,128)(2,1)S(1)}, u32[]{:S(2)}, u32[]{:S(2)}) %collective-permute-start.9) | collective-permute-done | bytes 1130528 | tf_op jit(solution)/shard_map/ppermute | solution.py:478
  151.5 3.4 multiply_reduce_fusion.2
  157.2 9.2 %attend_back.1 = (bf16[384,256]{1,0:T(8,128)(2,1)S(1)}, bf16[2688,384]{1,0:T(8,128)(2,1)S(1)}, f32[1,2688]{1,0:T(1,128)S(1)}, f32[3,512]{1,0:T(4,128)S(1)}, f32[6,128]{1,0:T(8,128)S(1)}) custom-call(bf16[384,256]{1,0:T(8,128)(2,1)S(1)} %convolution_convert_fusion.13.q_ref, bf16[2688,384]{1,0:T(8,128)(2,1)S(1)} %constant_dynamic-update-slice_fusion.kv_ref, ...), custom_call_target="tpu_custom_call" | custom-call | tf_op jit(solution)/shard_map/attend_back/pallas_call | solution.py:371
  166.4 4.9 %fusion.14 = bf16[384,1536]{1,0:T(8,128)(2,1)} fusion(s32[1536]{0:T(1024)S(1)} %copy-done.19, f32[384,1472]{0,1:T(8,128)} %copy-done), kind=kOutput, calls=%fused_computation.30 | convolution fusion | flops 1739857920 | bytes 3446784 | tf_op jit(solution)/shard_map/dot_general | solution.py:44
  175.8 9.4 %collective-permute-start.12 = (bf16[384,384]{1,0:T(8,128)(2,1)}, bf16[384,384]{1,0:T(8,128)(2,1)}, u32[]{:S(2)}, u32[]{:S(2)}) collective-permute-start(bf16[384,384]{1,0:T(8,128)(2,1)} %get-tuple-element.115), channel_id=1, source_target_pairs={{0,4},{4,8},{6,10},{10,14},{16,20},{20,24},{22,26},{26,30},{1,5},{... | collective-permute-start | bytes 884744 | tf_op jit(solution)/shard_map/ppermute | solution.py:395
  187.1 2.2 convolution_convert_fusion.10
  189.3 3.8 collective-permute-start.10
  194.2 1.5 convolution_convert_fusion.11
  195.7 1.9 collective-permute-start.25
  198.1 1.7 add_convert_fusion.22
  201.4 1.6 collective-permute-start.16
  203.5 2.7 collective-permute-start.22
  207.1 2.6 collective-permute-done.22
  209.8 3.2 collective-permute-start.23
  213.0 2.0 maximum_multiply_fusion
  217.3 3.5 collective-permute-done.24
  223.0 5.9 %collective-permute-done.16 = bf16[384,1472]{0,1:T(8,128)(2,1)S(1)} collective-permute-done((bf16[384,1472]{0,1:T(8,128)(2,1)S(1)}, bf16[384,1472]{0,1:T(8,128)(2,1)S(1)}, u32[]{:S(2)}, u32[]{:S(2)}) %collective-permute-start.16) | collective-permute-done | bytes 1130528 | tf_op jit(solution)/shard_map/ppermute | solution.py:478
  230.0 41.5 %psum.7 = f32[9283]{0:T(1024)S(1)} all-reduce(f32[9283]{0:T(1024)S(1)} %concatenate.27), channel_id=1, replica_groups=mesh['ctx'=16,'wt'=2] {'ctx','wt'}, use_global_device_ids=true, to_apply=%region_11.12 | all-reduce | flops 9283 | bytes 74264 | tf_op jit(solution)/shard_map/psum | solution.py:564
  271.6 3.4 fusion.30
  279.6 4.5 %add_convert_fusion.5 = (bf16[384,1792]{1,0:T(8,128)(2,1)S(1)}, bf16[384,1792]{1,0:T(8,128)(2,1)}) fusion(bf16[768,1792]{1,0:T(8,128)(2,1)} %collective-permute-done.25, bf16[768,1792]{1,0:T(8,128)(2,1)} %convolution_convert_fusion.5), kind=kLoop, calls=%fused_computation.45 | loop fusion | flops 5505024 | bytes 8257536 | tf_op jit(solution)/shard_map/convert_element_type | solution.py:442
  284.1 2.3 collective-permute-start.26
  286.3 3.7 add_convert_fusion.3
  290.2 2.2 collective-permute-start.20
  292.4 4.0 add_convert_fusion.1
  296.4 2.0 collective-permute-start.34
  301.2 16.5 %collective-permute-done.26 = bf16[384,1792]{1,0:T(8,128)(2,1)} collective-permute-done((bf16[384,1792]{1,0:T(8,128)(2,1)}, bf16[384,1792]{1,0:T(8,128)(2,1)}, u32[]{:S(2)}, u32[]{:S(2)}) %collective-permute-start.26) | collective-permute-done | bytes 1376288 | tf_op jit(solution)/shard_map/ppermute | solution.py:437
  317.7 1.6 add_convert_fusion.11
  319.4 2.1 collective-permute-start.27
  321.5 25.8 %collective-permute-done.30 = bf16[384,1792]{1,0:T(8,128)(2,1)} collective-permute-done((bf16[384,1792]{1,0:T(8,128)(2,1)}, bf16[384,1792]{1,0:T(8,128)(2,1)}, u32[]{:S(2)}, u32[]{:S(2)}) %collective-permute-start.30) | collective-permute-done | bytes 1376288 | tf_op jit(solution)/shard_map/ppermute | solution.py:437
  347.2 1.6 add_convert_fusion.9
  348.9 2.1 collective-permute-start.31
  350.9 24.1 %collective-permute-done.34 = bf16[384,1792]{1,0:T(8,128)(2,1)} collective-permute-done((bf16[384,1792]{1,0:T(8,128)(2,1)}, bf16[384,1792]{1,0:T(8,128)(2,1)}, u32[]{:S(2)}, u32[]{:S(2)}) %collective-permute-start.34) | collective-permute-done | bytes 1376288 | tf_op jit(solution)/shard_map/ppermute | solution.py:437
  375.1 1.7 add_convert_fusion.7
  376.8 1.8 collective-permute-start.35
  379.4 2.4 collective-permute-start.32
  381.9 24.3 %collective-permute-done.35 = bf16[192,1792]{1,0:T(8,128)(2,1)S(1)} collective-permute-done((bf16[192,1792]{1,0:T(8,128)(2,1)S(1)}, bf16[192,1792]{1,0:T(8,128)(2,1)S(1)}, u32[]{:S(2)}, u32[]{:S(2)}) %collective-permute-start.35) | collective-permute-done | bytes 688160 | tf_op jit(solution)/shard_map/ppermute | solution.py:437
  407.7 10.6 %collective-permute-done.32 = bf16[96,1792]{1,0:T(8,128)(2,1)S(1)} collective-permute-done((bf16[96,1792]{1,0:T(8,128)(2,1)S(1)}, bf16[96,1792]{1,0:T(8,128)(2,1)S(1)}, u32[]{:S(2)}, u32[]{:S(2)}) %collective-permute-start.32) | collective-permute-done | bytes 344096 | tf_op jit(solution)/shard_map/ppermute | solution.py:437
  419.2 5.2 %collective-permute-done.36 = bf16[96,1792]{1,0:T(8,128)(2,1)S(1)} collective-permute-done((bf16[96,1792]{1,0:T(8,128)(2,1)S(1)}, bf16[96,1792]{1,0:T(8,128)(2,1)S(1)}, u32[]{:S(2)}, u32[]{:S(2)}) %collective-permute-start.36) | collective-permute-done | bytes 344096 | tf_op jit(solution)/shard_map/ppermute | solution.py:437
  (233 shorter events, 47.7 us)
Async XLA Ops:
  2.5 16.2 %copy-start.26 = (bf16[1472,192]{0,1:T(8,128)(2,1)S(1)}, bf16[1472,192]{0,1:T(8,128)(2,1)}, u32[]{:S(2)}) copy-start(bf16[1472,192]{0,1:T(8,128)(2,1)} %param.19) | copy-start | bytes 1695748
  4.7 14.7 %copy-start.22 = (bf16[384]{0:T(512)(128)(2,1)S(1)}, bf16[384]{0:T(512)(128)(2,1)}, u32[]{:S(2)}) copy-start(bf16[384]{0:T(512)(128)(2,1)} %param.17) | copy-start | bytes 2308
  4.8 38.0 %copy-start.29 = (s32[16]{0:T(128)S(1)}, s32[16]{0:T(128)}, u32[]{:S(2)}) copy-start(s32[16]{0:T(128)} %constant.119.clone) | copy-start | bytes 196
  4.8 46.7 %collective-permute-start = (bf16[384,384]{1,0:T(8,128)(2,1)S(1)}, bf16[384,384]{1,0:T(8,128)(2,1)}, u32[]{:S(2)}, u32[]{:S(2)}) collective-permute-start(bf16[384,384]{1,0:T(8,128)(2,1)S(1)} %convolution_convert_fusion.12), channel_id=1, source_target_pairs={{4,10},{20,26},{5,11},{21,27}} | collective-permute-start | bytes 884744 | tf_op jit(solution)/shard_map/ppermute | solution.py:340
  6.2 47.2 %collective-permute-start.1 = (bf16[384,384]{1,0:T(8,128)(2,1)S(1)}, bf16[384,384]{1,0:T(8,128)(2,1)}, u32[]{:S(2)}, u32[]{:S(2)}) collective-permute-start(bf16[384,384]{1,0:T(8,128)(2,1)S(1)} %convolution_convert_fusion.12), channel_id=1, source_target_pairs={{0,4},{4,8},{6,10},{10,14},{16,20},{20,24},{22,26},{26,30},{1,5},{... | collective-permute-start | bytes 884744 | tf_op jit(solution)/shard_map/ppermute | solution.py:340
  14.0 42.0 %collective-permute-start.2 = (bf16[384,384]{1,0:T(8,128)(2,1)S(1)}, bf16[384,384]{1,0:T(8,128)(2,1)}, u32[]{:S(2)}, u32[]{:S(2)}) collective-permute-start(bf16[384,384]{1,0:T(8,128)(2,1)S(1)} %convolution_convert_fusion.12), channel_id=1, source_target_pairs={{0,2},{2,4},{4,6},{6,8},{8,10},{10,12},{12,14},{16,18},{18,20},{20... | collective-permute-start | bytes 884744 | tf_op jit(solution)/shard_map/ppermute | solution.py:340
  16.0 41.0 %collective-permute-start.3 = (bf16[384,384]{1,0:T(8,128)(2,1)S(1)}, bf16[384,384]{1,0:T(8,128)(2,1)}, u32[]{:S(2)}, u32[]{:S(2)}) collective-permute-start(bf16[384,384]{1,0:T(8,128)(2,1)S(1)} %convolution_convert_fusion.12), channel_id=1, source_target_pairs={{2,0},{4,2},{6,4},{8,6},{10,8},{12,10},{14,12},{18,16},{20,18},{22... | collective-permute-start | bytes 884744 | tf_op jit(solution)/shard_map/ppermute | solution.py:340
  17.3 40.8 %collective-permute-start.4 = (bf16[384,384]{1,0:T(8,128)(2,1)S(1)}, bf16[384,384]{1,0:T(8,128)(2,1)}, u32[]{:S(2)}, u32[]{:S(2)}) collective-permute-start(bf16[384,384]{1,0:T(8,128)(2,1)S(1)} %convolution_convert_fusion.12), channel_id=1, source_target_pairs={{4,0},{8,4},{10,6},{14,10},{20,16},{24,20},{26,22},{30,26},{5,1},{... | collective-permute-start | bytes 884744 | tf_op jit(solution)/shard_map/ppermute | solution.py:340
  43.0 32.2 %copy-start.18 = (s32[1536]{0:T(1024)}, s32[1536]{0:T(1024)S(1)}, u32[]{:S(2)}) copy-start(s32[1536]{0:T(1024)S(1)} %select_n.81) | copy-start | bytes 18436
  46.3 7.1 %copy-start.9 = (bf16[192,1472]{1,0:T(8,128)(2,1)S(1)}, bf16[192,1472]{1,0:T(8,128)(2,1)}, u32[]{:S(2)}) copy-start(bf16[192,1472]{1,0:T(8,128)(2,1)} %param.22) | copy-start | bytes 1695748
  51.5 7.6 %collective-permute-start.5 = (bf16[384,384]{1,0:T(8,128)(2,1)S(1)}, bf16[384,384]{1,0:T(8,128)(2,1)S(1)}, u32[]{:S(2)}, u32[]{:S(2)}) collective-permute-start(bf16[384,384]{1,0:T(8,128)(2,1)S(1)} %convolution_convert_fusion.12), channel_id=1, source_target_pairs={{10,4},{26,20},{11,5},{27,21}} | collective-permute-start | bytes 884744 | tf_op jit(solution)/shard_map/ppermute | solution.py:340
  53.4 19.8 %collective-permute-start.7 = (bf16[192,1472]{1,0:T(8,128)(2,1)S(1)}, bf16[192,1472]{1,0:T(8,128)(2,1)S(1)}, u32[]{:S(2)}, u32[]{:S(2)}) collective-permute-start(bf16[192,1472]{1,0:T(8,128)(2,1)S(1)} %copy-done.9), channel_id=1, source_target_pairs={{0,1},{1,0},{2,3},{3,2},{4,5},{5,4},{6,7},{7,6},{8,9},{9,8},{10,11... | collective-permute-start | bytes 1695752 | tf_op jit(solution)/shard_map/ppermute | solution.py:478
  64.4 10.4 %copy-start.11 = (bf16[384,128]{1,0:T(8,128)(2,1)}, bf16[384,128]{1,0:T(8,128)(2,1)S(1)}, u32[]{:S(2)}) copy-start(bf16[384,128]{1,0:T(8,128)(2,1)S(1)} %slice.313) | copy-start | bytes 294916
  64.4 8.8 %collective-permute-start.6 = (bf16[384,192]{1,0:T(8,128)(2,1)S(1)}, bf16[384,192]{1,0:T(8,128)(2,1)S(1)}, u32[]{:S(2)}, u32[]{:S(2)}) collective-permute-start(bf16[384,192]{1,0:T(8,128)(2,1)S(1)} %pad_maximum_fusion.1), channel_id=1, source_target_pairs={{0,1},{1,0},{2,3},{3,2},{4,5},{5,4},{6,7},{7,6},{8,9},{9,8},{10,11... | collective-permute-start | bytes 442376 | tf_op jit(solution)/shard_map/ppermute | solution.py:478
  65.6 9.2 %copy-start.15 = (f32[1472]{0:T(1024)S(1)}, f32[1472]{0:T(1024)}, u32[]{:S(2)}) copy-start(f32[1472]{0:T(1024)} %param.28) | copy-start | bytes 17668
  74.8 6.1 %slice-start.2 = ((s8[5275648]{0:T(1024)(128)(4,1)}), s8[4194304]{0:T(1024)(128)(4,1)S(1)}, s32[]{:S(2)}) async-start(s8[5275648]{0:T(1024)(128)(4,1)} %bitcast.44), calls=%async_computation.2 | async-start | bytes 8388608
  75.1 5.8 %slice-start.3 = ((s8[5275648]{0:T(1024)(128)(4,1)}), s8[1081344]{0:T(1024)(128)(4,1)S(1)}, s32[]{:S(2)}) async-start(s8[5275648]{0:T(1024)(128)(4,1)} %bitcast.44), calls=%async_computation.3 | async-start | bytes 2162688
  78.6 5.3 %slice-start.6 = ((s8[5275648]{0:T(1024)(128)(4,1)}), s8[4194304]{0:T(1024)(128)(4,1)S(1)}, s32[]{:S(2)}) async-start(s8[5275648]{0:T(1024)(128)(4,1)} %bitcast.47), calls=%async_computation.6 | async-start | bytes 8388608
  100.9 27.9 %collective-permute-start.8 = (bf16[384,1472]{0,1:T(8,128)(2,1)S(1)}, bf16[384,1472]{0,1:T(8,128)(2,1)S(1)}, u32[]{:S(2)}, u32[]{:S(2)}) collective-permute-start(bf16[384,1472]{0,1:T(8,128)(2,1)S(1)} %convolution_convert_fusion.7), channel_id=1, source_target_pairs={{0,1},{1,0},{2,3},{3,2},{4,5},{5,4},{6,7},{7,6},{8,9},{9,8},{10,11... | collective-permute-start | bytes 3391496 | tf_op jit(solution)/shard_map/ppermute | solution.py:478
  105.4 46.1 %collective-permute-start.9 = (bf16[384,1472]{0,1:T(8,128)(2,1)S(1)}, bf16[384,1472]{0,1:T(8,128)(2,1)S(1)}, u32[]{:S(2)}, u32[]{:S(2)}) collective-permute-start(bf16[384,1472]{0,1:T(8,128)(2,1)S(1)} %fusion.12), channel_id=1, source_target_pairs={{0,1},{1,0},{2,3},{3,2},{4,5},{5,4},{6,7},{7,6},{8,9},{9,8},{10,11... | collective-permute-start | bytes 3391496 | tf_op jit(solution)/shard_map/ppermute | solution.py:478
  156.3 10.1 %copy-start.19 = (s32[1536]{0:T(1024)S(1)}, s32[1536]{0:T(1024)}, u32[]{:S(2)}) copy-start(s32[1536]{0:T(1024)} %copy-done.18) | copy-start | bytes 18436
  171.3 15.5 %copy-start.23 = (f32[32]{0:T(128)S(1)}, f32[32]{0:T(128)}, u32[]{:S(2)}) copy-start(f32[32]{0:T(128)} %get-tuple-element.130) | copy-start | bytes 388
  171.3 15.5 %copy-start.24 = (f32[32]{0:T(128)S(1)}, f32[32]{0:T(128)}, u32[]{:S(2)}) copy-start(f32[32]{0:T(128)} %get-tuple-element.131) | copy-start | bytes 388
  171.3 15.8 %copy-start.12 = (bf16[384,128]{1,0:T(8,128)(2,1)S(1)}, bf16[384,128]{1,0:T(8,128)(2,1)}, u32[]{:S(2)}) copy-start(bf16[384,128]{1,0:T(8,128)(2,1)} %copy-done.11) | copy-start | bytes 294916
  171.3 21.8 %copy-start.25 = (pred[2]{0:T(512)(128)(4,1)S(1)}, pred[2]{0:T(512)(128)(4,1)}, u32[]{:S(2)}) copy-start(pred[2]{0:T(512)(128)(4,1)} %iota_compare_fusion.19) | copy-start | bytes 10
  172.4 16.8 %collective-permute-start.15 = (bf16[384,384]{1,0:T(8,128)(2,1)S(1)}, bf16[384,384]{1,0:T(8,128)(2,1)S(1)}, u32[]{:S(2)}, u32[]{:S(2)}) collective-permute-start(bf16[384,384]{1,0:T(8,128)(2,1)S(1)} %get-tuple-element.112), channel_id=1, source_target_pairs={{10,4},{26,20},{11,5},{27,21}} | collective-permute-start | bytes 884744 | tf_op jit(solution)/shard_map/ppermute | solution.py:395
  173.1 22.6 %collective-permute-start.14 = (bf16[384,384]{1,0:T(8,128)(2,1)}, bf16[384,384]{1,0:T(8,128)(2,1)}, u32[]{:S(2)}, u32[]{:S(2)}) collective-permute-start(bf16[384,384]{1,0:T(8,128)(2,1)} %get-tuple-element.113), channel_id=1, source_target_pairs={{4,10},{20,26},{5,11},{21,27}} | collective-permute-start | bytes 884744 | tf_op jit(solution)/shard_map/ppermute | solution.py:395
  174.5 23.1 %collective-permute-start.13 = (bf16[384,384]{1,0:T(8,128)(2,1)}, bf16[384,384]{1,0:T(8,128)(2,1)}, u32[]{:S(2)}, u32[]{:S(2)}) collective-permute-start(bf16[384,384]{1,0:T(8,128)(2,1)} %get-tuple-element.114), channel_id=1, source_target_pairs={{4,0},{8,4},{10,6},{14,10},{20,16},{24,20},{26,22},{30,26},{5,1},{... | collective-permute-start | bytes 884744 | tf_op jit(solution)/shard_map/ppermute | solution.py:395
  175.8 21.9 %collective-permute-start.12 = (bf16[384,384]{1,0:T(8,128)(2,1)}, bf16[384,384]{1,0:T(8,128)(2,1)}, u32[]{:S(2)}, u32[]{:S(2)}) collective-permute-start(bf16[384,384]{1,0:T(8,128)(2,1)} %get-tuple-element.115), channel_id=1, source_target_pairs={{0,4},{4,8},{6,10},{10,14},{16,20},{20,24},{22,26},{26,30},{1,5},{... | collective-permute-start | bytes 884744 | tf_op jit(solution)/shard_map/ppermute | solution.py:395
  185.2 13.0 %collective-permute-start.11 = (bf16[384,384]{1,0:T(8,128)(2,1)}, bf16[384,384]{1,0:T(8,128)(2,1)}, u32[]{:S(2)}, u32[]{:S(2)}) collective-permute-start(bf16[384,384]{1,0:T(8,128)(2,1)} %get-tuple-element.116), channel_id=1, source_target_pairs={{2,0},{4,2},{6,4},{8,6},{10,8},{12,10},{14,12},{18,16},{20,18},{22... | collective-permute-start | bytes 884744 | tf_op jit(solution)/shard_map/ppermute | solution.py:395
  189.3 8.8 %collective-permute-start.10 = (bf16[384,384]{1,0:T(8,128)(2,1)}, bf16[384,384]{1,0:T(8,128)(2,1)}, u32[]{:S(2)}, u32[]{:S(2)}) collective-permute-start(bf16[384,384]{1,0:T(8,128)(2,1)} %get-tuple-element.111), channel_id=1, source_target_pairs={{0,2},{2,4},{4,6},{6,8},{8,10},{10,12},{12,14},{16,18},{18,20},{20... | collective-permute-start | bytes 884744 | tf_op jit(solution)/shard_map/ppermute | solution.py:395
  193.5 6.4 %copy-start.13 = (bf16[1472,192]{0,1:T(8,128)(2,1)S(1)}, bf16[1472,192]{0,1:T(8,128)(2,1)}, u32[]{:S(2)}) copy-start(bf16[1472,192]{0,1:T(8,128)(2,1)} %param.21) | copy-start | bytes 1695748
  194.2 5.8 %copy-start.27 = (bf16[1472,192]{0,1:T(8,128)(2,1)S(1)}, bf16[1472,192]{0,1:T(8,128)(2,1)}, u32[]{:S(2)}) copy-start(bf16[1472,192]{0,1:T(8,128)(2,1)} %param.19) | copy-start | bytes 1695748
  194.2 5.8 %copy-start.28 = (bf16[1472,192]{0,1:T(8,128)(2,1)S(1)}, bf16[1472,192]{0,1:T(8,128)(2,1)}, u32[]{:S(2)}) copy-start(bf16[1472,192]{0,1:T(8,128)(2,1)} %param.20) | copy-start | bytes 1695748
  195.7 83.8 %collective-permute-start.25 = (bf16[768,1792]{1,0:T(8,128)(2,1)}, bf16[768,1792]{1,0:T(8,128)(2,1)}, u32[]{:S(2)}, u32[]{:S(2)}) collective-permute-start(bf16[768,1792]{1,0:T(8,128)(2,1)} %convolution_convert_fusion.4), channel_id=1, source_target_pairs={{0,2},{2,0},{4,6},{6,4},{8,10},{10,8},{12,14},{14,12},{16,18},{18,... | collective-permute-start | bytes 8257544 | tf_op jit(solution)/shard_map/ppermute | solution.py:437
  197.6 88.7 %collective-permute-start.29 = (bf16[768,1792]{1,0:T(8,128)(2,1)}, bf16[768,1792]{1,0:T(8,128)(2,1)}, u32[]{:S(2)}, u32[]{:S(2)}) collective-permute-start(bf16[768,1792]{1,0:T(8,128)(2,1)} %convolution_convert_fusion.2), channel_id=1, source_target_pairs={{0,2},{2,0},{4,6},{6,4},{8,10},{10,8},{12,14},{14,12},{16,18},{18,... | collective-permute-start | bytes 8257544 | tf_op jit(solution)/shard_map/ppermute | solution.py:437
  197.7 5.7 %collective-permute-start.21 = (bf16[768,192]{0,1:T(8,128)(2,1)}, bf16[768,192]{0,1:T(8,128)(2,1)S(1)}, u32[]{:S(2)}, u32[]{:S(2)}) collective-permute-start(bf16[768,192]{0,1:T(8,128)(2,1)} %convolution_convert_fusion.10), channel_id=1, source_target_pairs={{0,2},{2,0},{4,6},{6,4},{8,10},{10,8},{12,14},{14,12},{16,18},{18,... | collective-permute-start | bytes 884744 | tf_op jit(solution)/shard_map/ppermute | solution.py:437
  200.0 6.1 %copy-start.30 = (bf16[384,1536]{1,0:T(8,128)(2,1)S(1)}, bf16[384,1536]{1,0:T(8,128)(2,1)}, u32[]{:S(2)}) copy-start(bf16[384,1536]{1,0:T(8,128)(2,1)} %fusion.13) | copy-start | bytes 3538948
  201.4 27.6 %copy-start.5 = (bf16[384,1472]{0,1:T(8,128)(2,1)}, bf16[384,1472]{0,1:T(8,128)(2,1)S(1)}, u32[]{:S(2)}) copy-start(bf16[384,1472]{0,1:T(8,128)(2,1)S(1)} %convolution_convert_fusion.6) | copy-start | bytes 3391492
  201.4 27.6 %collective-permute-start.16 = (bf16[384,1472]{0,1:T(8,128)(2,1)S(1)}, bf16[384,1472]{0,1:T(8,128)(2,1)S(1)}, u32[]{:S(2)}, u32[]{:S(2)}) collective-permute-start(bf16[384,1472]{0,1:T(8,128)(2,1)S(1)} %convolution_convert_fusion.6), channel_id=1, source_target_pairs={{0,1},{1,0},{2,3},{3,2},{4,5},{5,4},{6,7},{7,6},{8,9},{9,8},{10,11... | collective-permute-start | bytes 3391496 | tf_op jit(solution)/shard_map/ppermute | solution.py:478
  203.5 6.2 %collective-permute-start.22 = (bf16[384,192]{0,1:T(8,128)(2,1)S(1)}, bf16[384,192]{0,1:T(8,128)(2,1)S(1)}, u32[]{:S(2)}, u32[]{:S(2)}) collective-permute-start(bf16[384,192]{0,1:T(8,128)(2,1)S(1)} %get-tuple-element.122), channel_id=1, source_target_pairs={{0,4},{2,6},{4,0},{6,2},{8,12},{10,14},{12,8},{14,10},{16,20},{18,... | collective-permute-start | bytes 442376 | tf_op jit(solution)/shard_map/ppermute | solution.py:437
  207.0 14.4 %collective-permute-start.17 = (bf16[768,576]{0,1:T(8,128)(2,1)S(1)}, bf16[768,576]{0,1:T(8,128)(2,1)S(1)}, u32[]{:S(2)}, u32[]{:S(2)}) collective-permute-start(bf16[768,576]{0,1:T(8,128)(2,1)S(1)} %convolution_convert_fusion.8), channel_id=1, source_target_pairs={{0,2},{2,0},{4,6},{6,4},{8,10},{10,8},{12,14},{14,12},{16,18},{18,... | collective-permute-start | bytes 2654216 | tf_op jit(solution)/shard_map/ppermute | solution.py:437
  209.8 5.8 %collective-permute-start.23 = (bf16[192,192]{0,1:T(8,128)(2,1)S(1)}, bf16[192,192]{0,1:T(8,128)(2,1)S(1)}, u32[]{:S(2)}, u32[]{:S(2)}) collective-permute-start(bf16[192,192]{0,1:T(8,128)(2,1)S(1)} %get-tuple-element.124), channel_id=1, source_target_pairs={{0,8},{2,10},{4,12},{6,14},{8,0},{10,2},{12,4},{14,6},{16,24},{18,... | collective-permute-start | bytes 221192 | tf_op jit(solution)/shard_map/ppermute | solution.py:437
  215.7 5.1 %collective-permute-start.24 = (bf16[96,192]{0,1:T(8,128)(2,1)S(1)}, bf16[96,192]{0,1:T(8,128)(2,1)S(1)}, u32[]{:S(2)}, u32[]{:S(2)}) collective-permute-start(bf16[96,192]{0,1:T(8,128)(2,1)S(1)} %add_convert_fusion.29), channel_id=1, source_target_pairs={{0,16},{2,18},{4,20},{6,22},{8,24},{10,26},{12,28},{14,30},{16,0},... | collective-permute-start | bytes 110600 | tf_op jit(solution)/shard_map/ppermute | solution.py:437
  217.2 11.7 %copy-start.3 = (bf16[384,1472]{0,1:T(8,128)(2,1)S(1)}, bf16[384,1472]{0,1:T(8,128)(2,1)}, u32[]{:S(2)}) copy-start(bf16[384,1472]{0,1:T(8,128)(2,1)} %param.16) | copy-start | bytes 3391492
  220.8 71.6 %collective-permute-start.33 = (bf16[768,1792]{1,0:T(8,128)(2,1)}, bf16[768,1792]{1,0:T(8,128)(2,1)}, u32[]{:S(2)}, u32[]{:S(2)}) collective-permute-start(bf16[768,1792]{1,0:T(8,128)(2,1)} %convolution_convert_fusion), channel_id=1, source_target_pairs={{0,2},{2,0},{4,6},{6,4},{8,10},{10,8},{12,14},{14,12},{16,18},{18,... | collective-permute-start | bytes 8257544 | tf_op jit(solution)/shard_map/ppermute | solution.py:437
  222.6 7.4 %copy-start.17 = (f32[1472]{0:T(1024)S(1)}, f32[1472]{0:T(1024)}, u32[]{:S(2)}) copy-start(f32[1472]{0:T(1024)} %get-tuple-element.91) | copy-start | bytes 17668
  222.6 7.4 %copy-start.20 = (f32[192]{0:T(256)S(1)}, f32[192]{0:T(256)}, u32[]{:S(2)}) copy-start(f32[192]{0:T(256)} %select_n.78) | copy-start | bytes 2308
  222.6 49.1 %copy-start.1 = (f32[384,1472]{0,1:T(8,128)S(1)}, f32[384,1472]{0,1:T(8,128)}, u32[]{:S(2)}) copy-start(f32[384,1472]{0,1:T(8,128)} %copy-done) | copy-start | bytes 6782980
  222.6 55.4 %collective-permute-start.18 = (bf16[384,576]{0,1:T(8,128)(2,1)}, bf16[384,576]{0,1:T(8,128)(2,1)}, u32[]{:S(2)}, u32[]{:S(2)}) collective-permute-start(bf16[384,576]{0,1:T(8,128)(2,1)} %get-tuple-element.118), channel_id=1, source_target_pairs={{0,4},{2,6},{4,0},{6,2},{8,12},{10,14},{12,8},{14,10},{16,20},{18,... | collective-permute-start | bytes 1327112 | tf_op jit(solution)/shard_map/ppermute | solution.py:437
  279.5 10.6 %collective-permute-start.19 = (bf16[192,576]{0,1:T(8,128)(2,1)S(1)}, bf16[192,576]{0,1:T(8,128)(2,1)S(1)}, u32[]{:S(2)}, u32[]{:S(2)}) collective-permute-start(bf16[192,576]{0,1:T(8,128)(2,1)S(1)} %get-tuple-element.120), channel_id=1, source_target_pairs={{0,8},{2,10},{4,12},{6,14},{8,0},{10,2},{12,4},{14,6},{16,24},{18,... | collective-permute-start | bytes 663560 | tf_op jit(solution)/shard_map/ppermute | solution.py:437
  279.6 6.8 %copy-start.8 = (bf16[768,1792]{1,0:T(8,128)(2,1)S(1)}, bf16[768,1792]{1,0:T(8,128)(2,1)}, u32[]{:S(2)}) copy-start(bf16[768,1792]{1,0:T(8,128)(2,1)} %convolution_convert_fusion.3) | copy-start | bytes 8257540
  284.1 33.7 %collective-permute-start.26 = (bf16[384,1792]{1,0:T(8,128)(2,1)}, bf16[384,1792]{1,0:T(8,128)(2,1)}, u32[]{:S(2)}, u32[]{:S(2)}) collective-permute-start(bf16[384,1792]{1,0:T(8,128)(2,1)} %get-tuple-element.99), channel_id=1, source_target_pairs={{0,4},{2,6},{4,0},{6,2},{8,12},{10,14},{12,8},{14,10},{16,20},{18,... | collective-permute-start | bytes 4128776 | tf_op jit(solution)/shard_map/ppermute | solution.py:437
  286.3 6.1 %copy-start.7 = (bf16[768,1792]{1,0:T(8,128)(2,1)S(1)}, bf16[768,1792]{1,0:T(8,128)(2,1)}, u32[]{:S(2)}) copy-start(bf16[768,1792]{1,0:T(8,128)(2,1)} %convolution_convert_fusion.1) | copy-start | bytes 8257540
  290.1 57.2 %collective-permute-start.30 = (bf16[384,1792]{1,0:T(8,128)(2,1)}, bf16[384,1792]{1,0:T(8,128)(2,1)}, u32[]{:S(2)}, u32[]{:S(2)}) collective-permute-start(bf16[384,1792]{1,0:T(8,128)(2,1)} %get-tuple-element.97), channel_id=1, source_target_pairs={{0,4},{2,6},{4,0},{6,2},{8,12},{10,14},{12,8},{14,10},{16,20},{18,... | collective-permute-start | bytes 4128776 | tf_op jit(solution)/shard_map/ppermute | solution.py:437
  290.2 8.7 %collective-permute-start.20 = (bf16[96,576]{0,1:T(8,128)(2,1)S(1)}, bf16[96,576]{0,1:T(8,128)(2,1)S(1)}, u32[]{:S(2)}, u32[]{:S(2)}) collective-permute-start(bf16[96,576]{0,1:T(8,128)(2,1)S(1)} %add_convert_fusion.25), channel_id=1, source_target_pairs={{0,16},{2,18},{4,20},{6,22},{8,24},{10,26},{12,28},{14,30},{16,0},... | collective-permute-start | bytes 331784 | tf_op jit(solution)/shard_map/ppermute | solution.py:437
  296.4 78.6 %collective-permute-start.34 = (bf16[384,1792]{1,0:T(8,128)(2,1)}, bf16[384,1792]{1,0:T(8,128)(2,1)}, u32[]{:S(2)}, u32[]{:S(2)}) collective-permute-start(bf16[384,1792]{1,0:T(8,128)(2,1)} %get-tuple-element.95), channel_id=1, source_target_pairs={{0,4},{2,6},{4,0},{6,2},{8,12},{10,14},{12,8},{14,10},{16,20},{18,... | collective-permute-start | bytes 4128776 | tf_op jit(solution)/shard_map/ppermute | solution.py:437
  319.4 55.7 %copy-start.4 = (bf16[384,1792]{1,0:T(8,128)(2,1)S(1)}, bf16[384,1792]{1,0:T(8,128)(2,1)}, u32[]{:S(2)}) copy-start(bf16[384,1792]{1,0:T(8,128)(2,1)} %get-tuple-element.94) | copy-start | bytes 4128772
  319.4 59.3 %collective-permute-start.27 = (bf16[192,1792]{1,0:T(8,128)(2,1)S(1)}, bf16[192,1792]{1,0:T(8,128)(2,1)S(1)}, u32[]{:S(2)}, u32[]{:S(2)}) collective-permute-start(bf16[192,1792]{1,0:T(8,128)(2,1)S(1)} %get-tuple-element.109), channel_id=1, source_target_pairs={{0,8},{2,10},{4,12},{6,14},{8,0},{10,2},{12,4},{14,6},{16,24},{18,... | collective-permute-start | bytes 2064392 | tf_op jit(solution)/shard_map/ppermute | solution.py:437
  348.9 30.5 %collective-permute-start.31 = (bf16[192,1792]{1,0:T(8,128)(2,1)S(1)}, bf16[192,1792]{1,0:T(8,128)(2,1)S(1)}, u32[]{:S(2)}, u32[]{:S(2)}) collective-permute-start(bf16[192,1792]{1,0:T(8,128)(2,1)S(1)} %get-tuple-element.107), channel_id=1, source_target_pairs={{0,8},{2,10},{4,12},{6,14},{8,0},{10,2},{12,4},{14,6},{16,24},{18,... | collective-permute-start | bytes 2064392 | tf_op jit(solution)/shard_map/ppermute | solution.py:437
  376.8 29.3 %collective-permute-start.35 = (bf16[192,1792]{1,0:T(8,128)(2,1)S(1)}, bf16[192,1792]{1,0:T(8,128)(2,1)S(1)}, u32[]{:S(2)}, u32[]{:S(2)}) collective-permute-start(bf16[192,1792]{1,0:T(8,128)(2,1)S(1)} %get-tuple-element.105), channel_id=1, source_target_pairs={{0,8},{2,10},{4,12},{6,14},{8,0},{10,2},{12,4},{14,6},{16,24},{18,... | collective-permute-start | bytes 2064392 | tf_op jit(solution)/shard_map/ppermute | solution.py:437
  378.7 28.0 %collective-permute-start.28 = (bf16[96,1792]{1,0:T(8,128)(2,1)S(1)}, bf16[96,1792]{1,0:T(8,128)(2,1)S(1)}, u32[]{:S(2)}, u32[]{:S(2)}) collective-permute-start(bf16[96,1792]{1,0:T(8,128)(2,1)S(1)} %add_convert_fusion.18), channel_id=1, source_target_pairs={{0,16},{2,18},{4,20},{6,22},{8,24},{10,26},{12,28},{14,30},{16,0},... | collective-permute-start | bytes 1032200 | tf_op jit(solution)/shard_map/ppermute | solution.py:437
  379.4 38.8 %collective-permute-start.32 = (bf16[96,1792]{1,0:T(8,128)(2,1)S(1)}, bf16[96,1792]{1,0:T(8,128)(2,1)S(1)}, u32[]{:S(2)}, u32[]{:S(2)}) collective-permute-start(bf16[96,1792]{1,0:T(8,128)(2,1)S(1)} %add_convert_fusion.16), channel_id=1, source_target_pairs={{0,16},{2,18},{4,20},{6,22},{8,24},{10,26},{12,28},{14,30},{16,0},... | collective-permute-start | bytes 1032200 | tf_op jit(solution)/shard_map/ppermute | solution.py:437
  406.2 18.2 %collective-permute-start.36 = (bf16[96,1792]{1,0:T(8,128)(2,1)S(1)}, bf16[96,1792]{1,0:T(8,128)(2,1)S(1)}, u32[]{:S(2)}, u32[]{:S(2)}) collective-permute-start(bf16[96,1792]{1,0:T(8,128)(2,1)S(1)} %add_convert_fusion.14), channel_id=1, source_target_pairs={{0,16},{2,18},{4,20},{6,22},{8,24},{10,26},{12,28},{14,30},{16,0},... | collective-permute-start | bytes 1032200 | tf_op jit(solution)/shard_map/ppermute | solution.py:437
  (13 other events, 32.8 us)
